TPU v7x, 512 devices: a whole 4x8x8 slice. The times are simulated.
512 devices in a mesh: ctx: 64 (over z, x, core), head: 8 (over y).
Axes of the slice: x: 4, y: 8, z: 8, core: 2. Of those that a mesh axis runs over, the one named last changes fastest.
Arguments:
- context_query: bfloat16 [32768, 8192], P('ctx', 'head'), may hold values from -15 to 15
- context_key: bfloat16 [32768, 1024], P('ctx', 'head'), may hold values from -6 to 6
- context_value: bfloat16 [32768, 1024], P('ctx', 'head'), may hold values from -6 to 6
- request_query: bfloat16 [16384, 8192], P('ctx', 'head'), may hold values from -15 to 15, as said below
- request_key: bfloat16 [16384, 1024], P('ctx', 'head'), may hold values from -6 to 6, as said below
- request_value: bfloat16 [16384, 1024], P('ctx', 'head'), may hold values from -6 to 6
- output_weight: bfloat16 [8192, 8192], P('head', 'ctx'), may hold values from -0.375 to 0.375
- block_lengths: int32 [64], replicated, may hold values from 1 to 512, 24576 in all
- query_host: int32 [1], replicated, may hold values from 0 to 63
Outputs:
- encoded_context: bfloat16 [32768, 8192], P('ctx', 'head')
- request_output: bfloat16 [256, 8192], P('head', 'ctx')
Inputs may be any that keep to these rules, and one draw needn't show every extreme that they name: `request_query`: only the slot of host query_host[0] is read. `request_key`: only the slot of host query_host[0] is read. `block_lengths`: one entry a host; the largest is exactly 512; together they are 24576.
All inputs are finite; a program needn't handle non-finite values.
Results may differ from a plain program's by a relative error of at most 0.019.
Values may be sent and summed in bfloat16 or wider, within the bound.
No kernel may reach another device: no remote copies, remote signals or barrier semaphores. Data moves between devices by JAX's collectives and lax.ppermute only.
A program may use at most 192 MiB of HBM per device.

v0:
```python
import jax
import jax.numpy as jnp
from jax import lax
from jax.sharding import PartitionSpec as P

HD = 128


def broadcast(value, axis, source):
    kept = jnp.where(lax.axis_index(axis) == source, value, 0).astype(value.dtype)
    return lax.psum(kept, axis)


def head_terms(queries, key_rows, value_rows, seen_mask):
    local_heads = queries.shape[1] // HD

    def one_head(head_index):
        query_head = lax.dynamic_slice_in_dim(queries, head_index * HD, HD, 1)
        scores = lax.dot_general(
            query_head, key_rows, (((1,), (1,)), ((), ())), preferred_element_type=jnp.float32
        ) * HD ** (-0.5)
        scores = jnp.where(seen_mask, scores, -jnp.inf)
        row_peak = jnp.max(scores, axis=1)
        weights = jnp.exp(scores - row_peak[:, None]).astype(jnp.bfloat16)
        row_total = jnp.sum(weights.astype(jnp.float32), axis=1)
        row_values = jnp.dot(weights, value_rows, preferred_element_type=jnp.float32)
        return (row_peak, row_total, row_values)

    return lax.map(one_head, jnp.arange(local_heads, dtype=jnp.int32))


def heads_to_rows(stacked):
    return stacked.transpose(1, 0, 2).reshape(stacked.shape[1], stacked.shape[0] * stacked.shape[2])


def body(
    context_query,
    context_key,
    context_value,
    request_query,
    request_key,
    request_value,
    output_weight,
    block_lengths,
    query_host,
):
    host_index = lax.axis_index("ctx")
    own_len = lax.dynamic_index_in_dim(block_lengths, host_index, 0, keepdims=False)
    anchor_len = block_lengths[0]
    anchor_key, anchor_value = (
        broadcast(context_key, "ctx", 0),
        broadcast(context_value, "ctx", 0),
    )
    row_count = context_query.shape[0]
    row_ids = lax.broadcasted_iota(jnp.int32, (row_count, row_count), 0)
    col_ids = lax.broadcasted_iota(jnp.int32, (row_count, row_count), 1)
    own_seen = (col_ids <= row_ids) & (col_ids < own_len)
    anchor_seen = (col_ids < anchor_len) & (host_index > 0)
    row_peak, row_total, row_values = head_terms(
        context_query,
        jnp.concatenate([anchor_key, context_key], axis=0),
        jnp.concatenate([anchor_value, context_value], axis=0),
        jnp.concatenate([anchor_seen, own_seen], axis=1),
    )
    encoded = heads_to_rows(row_values / row_total[:, :, None])
    live_rows = lax.broadcasted_iota(jnp.int32, (row_count, 1), 0) < own_len
    encoded_context = jnp.where(live_rows, encoded, 0.0).astype(jnp.bfloat16)
    slot_host = query_host[0]
    queries = broadcast(request_query, "ctx", slot_host)
    slot_count = queries.shape[0]
    block_seen = lax.broadcasted_iota(jnp.int32, (slot_count, row_count), 1) < own_len
    slot_rows = lax.broadcasted_iota(jnp.int32, (slot_count, slot_count), 0)
    slot_cols = lax.broadcasted_iota(jnp.int32, (slot_count, slot_count), 1)
    self_seen = (slot_cols <= slot_rows) & (host_index == slot_host)
    ask_peak, ask_total, ask_values = head_terms(
        queries,
        jnp.concatenate([context_key, request_key], axis=0),
        jnp.concatenate([context_value, request_value], axis=0),
        jnp.concatenate([block_seen, self_seen], axis=1),
    )
    global_peak = lax.pmax(ask_peak, "ctx")
    rescale = jnp.exp(ask_peak - global_peak)
    numer_sum, denom_sum = lax.psum((ask_values * rescale[:, :, None], ask_total * rescale), "ctx")
    merged = (numer_sum / denom_sum[:, :, None]).astype(jnp.bfloat16)
    attended = heads_to_rows(merged)
    request_output = lax.psum_scatter(
        jnp.dot(attended, output_weight, preferred_element_type=jnp.float32).astype(jnp.bfloat16),
        "head",
        scatter_dimension=0,
        tiled=True,
    )
    return (encoded_context, request_output)


def solution(mesh):
    placed = (
        P("ctx", "head"),
        P("ctx", "head"),
        P("ctx", "head"),
        P("ctx", "head"),
        P("ctx", "head"),
        P("ctx", "head"),
        P("head", "ctx"),
        P(),
        P(),
    )
    return jax.shard_map(
        body,
        mesh=mesh,
        in_specs=placed,
        out_specs=(P("ctx", "head"), P("head", "ctx")),
        check_vma=False,
    )
```

profile of v0, /device:TPU:1, one launch (start us, length us, event | category | flops | bytes accessed | tf_op | source)
XLA Modules:
  0.0 622.3 jit_solution(6558214999298570191)
XLA Ops:
  8.1 0.8 broadcast_select_fusion
  8.9 0.7 broadcast_select_fusion.1
  11.0 0.8 fusion.8
  12.7 1.2 pad_add_fusion
  13.8 198.6 %all-reduce.6.cloned.1.call-done = (bf16[512,128]{1,0:T(8,128)(2,1)}, bf16[512,128]{1,0:T(8,128)(2,1)}, bf16[256,1024]{1,0:T(8,128)(2,1)}) async-done(((bf16[512,128]{1,0:T(8,128)(2,1)}, bf16[512,128]{1,0:T(8,128)(2,1)}, bf16[256,1024]{1,0:T(8,128)(2,1)}), (bf16[512,128]{1,0:T(8,128)(2,1)}, bf16[512,128]{1,0:T(8,128)(2,1)}, bf16[256,1024]{1,0:T(8,128)(2,1)})) %all-reduce.6.cloned.1.call-update) | async-done | bytes 786448 | tf_op jit(solution)/shard_map/psum | solution.py:11
  212.4 42.1 %while.27 = (s32[]{:T(128)}, f32[8,256]{1,0:T(8,128)S(1)}, f32[8,256]{1,0:T(8,128)}, f32[8,256,128]{1,2,0:T(8,128)}, s32[8]{0:T(128)S(1)}, /*index=5*/bf16[256,1...) while((s32[]{:T(128)}, f32[8,256]{1,0:T(8,128)S(1)}, ...), condition=%wide.region_10.11_spmd, body=%wide.region_7.10_spmd.sunk | while | flops 102432256 | bytes 3154627 | solution.py:29
  213.8 1.2 fusion.35
  215.0 1.1 fusion.36
  216.3 1.3 dynamic_update_slice.30
  217.7 0.7 dynamic_slice.34
  219.1 1.2 fusion.35
  220.3 1.1 fusion.36
  221.6 1.3 dynamic_update_slice.30
  223.0 0.7 dynamic_slice.34
  224.3 1.2 fusion.35
  225.6 1.1 fusion.36
  226.9 1.3 dynamic_update_slice.30
  228.2 0.7 dynamic_slice.34
  229.6 1.2 fusion.35
  230.8 1.1 fusion.36
  232.2 1.3 dynamic_update_slice.30
  233.5 0.7 dynamic_slice.34
  234.9 1.2 fusion.35
  236.1 1.1 fusion.36
  237.4 1.3 dynamic_update_slice.30
  238.8 0.7 dynamic_slice.34
  240.1 1.2 fusion.35
  241.4 1.1 fusion.36
  242.7 1.3 dynamic_update_slice.30
  244.0 0.7 dynamic_slice.34
  245.4 1.2 fusion.35
  246.6 1.1 fusion.36
  248.0 1.3 dynamic_update_slice.30
  249.3 0.7 dynamic_slice.34
  250.7 1.2 fusion.35
  251.9 1.1 fusion.36
  253.2 1.3 dynamic_update_slice.30
  254.6 127.6 %pmax.7 = f32[8,256]{1,0:T(8,128)S(1)} all-reduce(f32[8,256]{1,0:T(8,128)S(1)} %get-tuple-element.97), channel_id=1, replica_groups=mesh['ctx'=64,'head'=8] {'ctx'}, use_global_device_ids=true, to_apply=%region_11.12 | all-reduce | flops 2048 | bytes 16384 | tf_op jit(solution)/shard_map/pmax | solution.py:81
  382.2 0.7 fusion.11
  382.9 2.3 broadcast_multiply_fusion
  385.3 0.9 pad_maximum_fusion.1
  386.2 40.7 %while.26 = (s32[]{:T(128)}, f32[8,512]{1,0:T(8,128)}, f32[8,512,128]{2,1,0:T(8,128)S(1)}, s32[8]{0:T(128)S(1)}, bf16[512,1024]{1,0:T(8,128)(2,1)}, /*index=5*/b...) while((s32[]{:T(128)}, f32[8,512]{1,0:T(8,128)}, ...), condition=%wide.region_5.6_spmd, body=%wide.region_2.5_spmd.sunk | while | flops 273153024 | bytes 7745723 | solution.py:29
  387.5 1.5 fusion.31
  390.0 1.3 dynamic_update_slice.27
  392.6 1.5 fusion.31
  395.1 1.3 dynamic_update_slice.27
  397.6 1.5 fusion.31
  400.2 1.3 dynamic_update_slice.27
  402.7 1.5 fusion.31
  405.2 1.3 dynamic_update_slice.27
  407.8 1.5 fusion.31
  410.3 1.3 dynamic_update_slice.27
  412.9 1.5 fusion.31
  415.4 1.3 dynamic_update_slice.27
  418.0 1.5 fusion.31
  420.5 1.3 dynamic_update_slice.27
  423.1 1.5 fusion.31
  425.6 1.3 dynamic_update_slice.27
  426.9 129.6 %psum.39 = f32[8,256]{1,0:T(8,128)S(1)} all-reduce(f32[8,256]{1,0:T(8,128)S(1)} %get-tuple-element.136), channel_id=1, replica_groups=mesh['ctx'=64,'head'=8] {'ctx'}, use_global_device_ids=true, to_apply=%region_13.14 | all-reduce | flops 2048 | bytes 16384 | tf_op jit(solution)/shard_map/psum | solution.py:83
  556.5 23.8 %all-reduce.4.cloned.1.call-done = f32[8,256,128]{1,2,0:T(8,128)} async-done(((f32[8,256,128]{1,2,0:T(8,128)}), f32[8,256,128]{1,2,0:T(8,128)}) %all-reduce.4.cloned.1.call-update) | async-done | bytes 1048592 | tf_op jit(solution)/shard_map/psum | solution.py:83
  580.3 1.3 divide_convert_fusion
  581.6 1.0 convolution_convert_fusion
  582.6 1.7 fusion.7
  584.3 31.5 %reduce-scatter.2.cloned.1.call-done = bf16[32,128]{1,0:T(8,128)(2,1)} async-done(((bf16[256,128]{1,0:T(8,128)(2,1)}), bf16[32,128]{1,0:T(8,128)(2,1)}) %reduce-scatter.2.cloned.1.call-update) | async-done | bytes 8208 | tf_op jit(solution)/shard_map/reduce_scatter | solution.py:86
  (87 shorter events, 18.1 us)
Async XLA Ops:
  7.2 574.4 %copy-start = (bf16[1024,128]{1,0:T(8,128)(2,1)S(1)}, bf16[1024,128]{1,0:T(8,128)(2,1)}, u32[]{:S(2)}) copy-start(bf16[1024,128]{1,0:T(8,128)(2,1)} %param.19) | copy-start | bytes 786436
  7.2 5.4 copy-start.1
  7.2 5.4 copy-start.3
  7.2 2.6 copy-start.11
  7.2 5.4 copy-start.6
  7.2 5.4 copy-start.7
  7.2 205.2 %all-reduce.6.cloned.1.call-start = ((), (), s32[]{:S(2)}) async-start(), calls=%async_computation.3 | async-start | bytes 1572864 | tf_op jit(solution)/shard_map/psum | solution.py:11
  9.7 570.6 %all-reduce.4.cloned.1.call-start = ((), (), s32[]{:S(2)}) async-start(), calls=%async_computation.1 | async-start | bytes 2097152 | tf_op jit(solution)/shard_map/psum | solution.py:83
  11.0 0.9 copy-start.9
  254.6 130.7 %copy-start.2 = (bf16[512,128]{1,0:T(8,128)(2,1)S(1)}, bf16[512,128]{1,0:T(8,128)(2,1)}, u32[]{:S(2)}) copy-start(bf16[512,128]{1,0:T(8,128)(2,1)} %param.14) | copy-start | bytes 393220
  254.6 130.7 %copy-start.5 = (bf16[512,128]{1,0:T(8,128)(2,1)S(1)}, bf16[512,128]{1,0:T(8,128)(2,1)}, u32[]{:S(2)}) copy-start(bf16[512,128]{1,0:T(8,128)(2,1)} %get-tuple-element.133) | copy-start | bytes 393220
  254.6 130.7 %copy-start.4 = (bf16[512,128]{1,0:T(8,128)(2,1)S(1)}, bf16[512,128]{1,0:T(8,128)(2,1)}, u32[]{:S(2)}) copy-start(bf16[512,128]{1,0:T(8,128)(2,1)} %param.15) | copy-start | bytes 393220
  385.2 230.6 %reduce-scatter.2.cloned.1.call-start = ((), (), s32[]{:S(2)}) async-start(), calls=%async_computation.2 | async-start | bytes 73728 | tf_op jit(solution)/shard_map/reduce_scatter | solution.py:86
  426.9 155.7 %copy-start.8 = (f32[8,512]{1,0:T(8,128)S(1)}, f32[8,512]{1,0:T(8,128)}, u32[]{:S(2)}) copy-start(f32[8,512]{1,0:T(8,128)} %get-tuple-element.95) | copy-start | bytes 49156
  426.9 155.7 %copy-start.10 = (pred[512]{0:T(512)(128)(4,1)S(1)}, pred[512]{0:T(512)(128)(4,1)}, u32[]{:S(2)}) copy-start(pred[512]{0:T(512)(128)(4,1)} %copy-done.9) | copy-start | bytes 1540
Sparse Core Ops, SparseCore 0:
  11.8 200.5 all-reduce.5
  385.3 194.9 all-reduce.3
  583.6 32.1 reduce-scatter.1
where the time goes:
time: 629 us; the launch traced here: 622 us
  blocking collectives  257 us (41%)
  waiting for transfers between devices  254 us (40%)
  matrix products  35.1 us (6%)
  local copies, waits for them, and re-layouts  32.1 us (5%)
  other arithmetic  18.1 us (3%)
  between operations  14.8 us (2%)
  loops' own time  11 us (2%)
    psum x1, waiting for transfers between devices, broadcast(): return lax.psum(kept, axis)  199 us
    psum x1, blocking collectives, body(): lax.psum((ask_values * rescale[:, :, None], ask_total * rescale), 'ctx')  130 us
    pmax x1, blocking collectives, body(): global_peak = lax.pmax(ask_peak, 'ctx')  128 us
    reduce_scatter x1, waiting for transfers between devices, body(): lax.psum_scatter(jnp.dot(attended, output_weight, preferred_element_type=...  31.5 us
    psum x1, waiting for transfers between devices, body(): lax.psum((ask_values * rescale[:, :, None], ask_total * rescale), 'ctx')  23.8 us
    dot_general x16, matrix products, one_head(): lax.dot_general(query_head, key_rows, (((1,), (1,)), ((), ())), preferred...  21.5 us
    dynamic_update_slice x24, local copies, waits for them, and re-layouts, head_terms(): return lax.map(one_head, jnp.arange(local_heads, dtype=jnp.int32))  21.4 us
    dot_general x16, matrix products, one_head(): jnp.dot(weights, value_rows, preferred_element_type=jnp.float32)  12.6 us
  transfers between devices with their start and end apart: 3, of which 3 were waited for; matrix products, arithmetic and copies ran while one was open for 7% of the time, Pallas kernels for 0%

commit v1 on v0

v1 whole, which is shorter than its diff:
```python
import jax
import jax.numpy as jnp
from jax import lax
from jax.experimental import pallas as pl
from jax.experimental.pallas import tpu as pltpu
from jax.sharding import Mesh, PartitionSpec as P

HD = 128
HEADS = 8
HALF = HEADS // 2
BLOCK = 512
QUERY = 256
Z, X, C = 8, 4, 2
SCALE = HD ** (-0.5) * 1.4426950408889634
NEG = -1e30
BF16 = jnp.bfloat16
F32 = jnp.float32
CHIPS = ("z", "x")


def params(**extra):
    return pltpu.CompilerParams(vmem_limit_bytes=32 * 1024 * 1024, **extra)


def smem():
    return pl.BlockSpec(memory_space=pltpu.SMEM)


def vmem():
    return pl.BlockSpec(memory_space=pltpu.VMEM)


def weigh(query, parts):
    scores = []
    for keys, _, seen in parts:
        score = lax.dot_general(query, keys, (((1,), (1,)), ((), ())), preferred_element_type=F32)
        scores.append(score if seen is None else jnp.where(seen, score, NEG))
    peak = scores[0].max(axis=1, keepdims=True)
    for score in scores[1:]:
        peak = jnp.maximum(peak, score.max(axis=1, keepdims=True))
    total = None
    for score, (_, values, _) in zip(scores, parts):
        weights = jnp.exp2((score - peak) * SCALE).astype(BF16)
        term = jnp.dot(weights, values, preferred_element_type=F32)
        total = term if total is None else total + term
    return peak, total[:, :HD], total[:, HD:]


def with_ones(values):
    return jnp.concatenate([values, jnp.ones(values.shape, BF16)], axis=1)


def column_ids(rows, cols):
    return lax.broadcasted_iota(jnp.int32, (rows, cols), 1)


def causal(size):
    return column_ids(size, size) <= lax.broadcasted_iota(jnp.int32, (size, size), 0)


def pack_kernel(query, key, value, ask_key, ask_value, to_core, to_pair):
    pieces, piece_rows = to_core.shape[1], HALF * QUERY // to_core.shape[1]
    per_head = pieces // HALF
    extra = BLOCK // pieces
    for core, rows in ((0, key), (1, value)):
        for head in range(HALF):
            column = (core * HALF + head) * HD
            to_core[core, head * per_head : (head + 1) * per_head, :piece_rows, :] = query[
                :, column : column + HD
            ].reshape(per_head, piece_rows, HD)
        to_core[core, :, piece_rows:, :] = rows[...].reshape(pieces, extra, HD)
    to_pair[0:BLOCK, :] = key[...]
    to_pair[BLOCK : 2 * BLOCK, :] = value[...]
    to_pair[2 * BLOCK : 2 * BLOCK + QUERY, :] = ask_key[...]
    to_pair[2 * BLOCK + QUERY :, :] = ask_value[...]


def pack(query, key, value, ask_key, ask_value, pieces):
    rows = (HALF * QUERY + BLOCK) // pieces
    return pl.pallas_call(
        pack_kernel,
        out_shape=(
            jax.ShapeDtypeStruct((C, pieces, rows, HD), BF16),
            jax.ShapeDtypeStruct((2 * BLOCK + 2 * QUERY, HD), BF16),
        ),
        in_specs=[vmem()] * 5,
        out_specs=(vmem(), vmem()),
        compiler_params=params(),
        name="pack",
    )(query, key, value, ask_key, ask_value)


def choose_kernel(which, asked, anchor, out):
    split = HALF * QUERY // (out.shape[-3])
    out[:, :split, :] = asked[0, :, :split, :]
    out[:, split:, :] = anchor[0, :, split:, :]


def choose(which, received):
    shape = received.shape[1:]
    return pl.pallas_call(
        choose_kernel,
        out_shape=jax.ShapeDtypeStruct(shape, BF16),
        grid_spec=pltpu.PrefetchScalarGridSpec(
            num_scalar_prefetch=1,
            grid=(1,),
            in_specs=[
                pl.BlockSpec((1,) + shape, lambda i, which: (which[0], 0, 0, 0)),
                pl.BlockSpec((1,) + shape, lambda i, which: (0, 0, 0, 0)),
            ],
            out_specs=pl.BlockSpec(shape, lambda i, which: (0, 0, 0)),
        ),
        compiler_params=params(),
        name="choose",
    )(which, received, received)


def spread_kernel(which, asked, anchor, out):
    split = HALF * QUERY // out.shape[0]
    out[:, :split, :] = jnp.broadcast_to(asked[:, :split, :], (out.shape[0], split, HD))
    out[:, split:, :] = jnp.broadcast_to(anchor[:, split:, :], (out.shape[0], out.shape[1] - split, HD))


def spread(which, received):
    pieces, rows, _ = received.shape
    return pl.pallas_call(
        spread_kernel,
        out_shape=jax.ShapeDtypeStruct(received.shape, BF16),
        grid_spec=pltpu.PrefetchScalarGridSpec(
            num_scalar_prefetch=1,
            grid=(1,),
            in_specs=[
                pl.BlockSpec((1, rows, HD), lambda i, which: (which[0], 0, 0)),
                pl.BlockSpec((1, rows, HD), lambda i, which: (0, 0, 0)),
            ],
            out_specs=pl.BlockSpec(received.shape, lambda i, which: (0, 0, 0)),
        ),
        compiler_params=params(),
        name="spread",
    )(which, received, received)


def ask_kernel(meta, query, rows, out, values):
    pieces, piece_rows = query.shape[0], HALF * QUERY // query.shape[0]
    per_head = pieces // HALF
    for core in range(C):
        values[core * BLOCK : (core + 1) * BLOCK, :] = with_ones(rows[core, BLOCK : 2 * BLOCK, :])

    def run(own):
        for head in range(HALF):
            asked = query[head * per_head : (head + 1) * per_head, :piece_rows, :].reshape(QUERY, HD)
            parts = [
                (
                    rows[core, 0:BLOCK, :],
                    values[core * BLOCK : (core + 1) * BLOCK, :],
                    column_ids(QUERY, BLOCK) < meta[core],
                )
                for core in range(C)
            ]
            if own:
                ask_key = rows[meta[3], 2 * BLOCK : 2 * BLOCK + QUERY, :]
                ask_value = with_ones(rows[meta[3], 2 * BLOCK + QUERY :, :])
                parts.append((ask_key, ask_value, causal(QUERY)))
            peak, numer, denom = weigh(asked, parts)
            out[head * per_head : (head + 1) * per_head, :piece_rows, :] = (
                (numer / denom).astype(BF16).reshape(per_head, piece_rows, HD)
            )
            level = peak * SCALE + jnp.log2(denom)
            high = level.astype(BF16)
            rest = level - high.astype(F32)
            middle = rest.astype(BF16)
            low = (rest - middle.astype(F32)).astype(BF16)
            lane = column_ids(QUERY, HD) % (HD // 2)
            coded = jnp.where(lane == 0, high.astype(F32), jnp.where(lane == 1, middle.astype(F32), low.astype(F32)))
            coded = coded.reshape(per_head, piece_rows, HD)
            left = column_ids(piece_rows // 2, HD) < HD // 2
            coded = jnp.where(left[None], coded[:, : piece_rows // 2, :], coded[:, piece_rows // 2 :, :])
            out[head * per_head : (head + 1) * per_head, piece_rows:, :] = coded.astype(BF16)

    @pl.when(meta[2] == 0)
    def _():
        run(False)

    @pl.when(meta[2] != 0)
    def _():
        run(True)


def ask(meta, query, rows):
    pieces = query.shape[0]
    piece_rows = HALF * QUERY // pieces
    return pl.pallas_call(
        ask_kernel,
        out_shape=jax.ShapeDtypeStruct((pieces, piece_rows + piece_rows // 2, HD), BF16),
        in_specs=[smem(), vmem(), vmem()],
        out_specs=vmem(),
        scratch_shapes=[pltpu.VMEM((C * BLOCK, 2 * HD), BF16)],
        compiler_params=params(),
        name="ask",
    )(meta, query, rows)


def merge_kernel(received, out):
    pieces, piece_rows = out.shape[0], out.shape[1]
    half = piece_rows // 2
    levels = []
    for piece in range(pieces):
        coded = received[piece, piece_rows:, :].astype(F32)
        first = coded[:, 0:1] + coded[:, 1:2] + coded[:, 2:3]
        second = coded[:, 64:65] + coded[:, 65:66] + coded[:, 66:67]
        levels.append(jnp.concatenate([first, second], axis=0))
    top = levels[0]
    for level in levels[1:]:
        top = jnp.maximum(top, level)
    numer = jnp.zeros((piece_rows, HD), F32)
    denom = jnp.zeros((piece_rows, 1), F32)
    for piece, level in enumerate(levels):
        share = jnp.exp2(level - top)
        numer += share * received[piece, :piece_rows, :].astype(F32)
        denom += share
    merged = (numer / denom).astype(BF16)
    out[...] = jnp.broadcast_to(merged[None], out.shape)


def merge(received):
    pieces = received.shape[0]
    return pl.pallas_call(
        merge_kernel,
        out_shape=jax.ShapeDtypeStruct((pieces, HALF * QUERY // pieces, HD), BF16),
        in_specs=[vmem()],
        out_specs=vmem(),
        compiler_params=params(),
        name="merge",
    )(received)


def project_kernel(attended, weight, out):
    total = jnp.zeros((QUERY, HD), F32)
    for head in range(HEADS):
        total += jnp.dot(
            attended[head * QUERY : (head + 1) * QUERY, :],
            weight[head * HD : (head + 1) * HD, :],
            preferred_element_type=F32,
        )
    out[...] = total.astype(BF16)


def project(attended, weight):
    return pl.pallas_call(
        project_kernel,
        out_shape=jax.ShapeDtypeStruct((QUERY, HD), BF16),
        in_specs=[vmem(), vmem()],
        out_specs=vmem(),
        compiler_params=params(),
        name="project",
    )(attended, weight)


def encode_kernel(meta, query, key, value, anchor, out, own_values, anchor_values):
    @pl.when(pl.program_id(0) == 0)
    def _():
        own_values[...] = with_ones(value[...])
        anchor_values[...] = with_ones(anchor[BLOCK:, :])

    own_len, anchor_len = meta[4], meta[5]
    half = BLOCK // 2
    for tile in range(2):
        rows = slice(tile * half, (tile + 1) * half)
        parts = [
            (key[rows, :], own_values[rows, :], causal(half)),
            (anchor[:BLOCK, :], anchor_values[...], column_ids(half, BLOCK) < anchor_len),
        ]
        if tile:
            parts.append((key[:half, :], own_values[:half, :], None))
        _, numer, denom = weigh(query[rows, :], parts)
        live = lax.broadcasted_iota(jnp.int32, (half, HD), 0) + tile * half < own_len
        out[rows, :] = jnp.where(live, numer / denom, 0.0).astype(BF16)


def encode(meta, query, key, value, anchor):
    return pl.pallas_call(
        encode_kernel,
        out_shape=jax.ShapeDtypeStruct(query.shape, BF16),
        grid=(HEADS,),
        in_specs=[
            smem(),
            pl.BlockSpec((BLOCK, HD), lambda h: (0, h)),
            pl.BlockSpec((BLOCK, HD), lambda h: (0, 0)),
            pl.BlockSpec((BLOCK, HD), lambda h: (0, 0)),
            pl.BlockSpec((2 * BLOCK, HD), lambda h: (0, 0)),
        ],
        out_specs=pl.BlockSpec((BLOCK, HD), lambda h: (0, h)),
        scratch_shapes=[pltpu.VMEM((BLOCK, 2 * HD), BF16)] * 2,
        compiler_params=params(),
        cost_estimate=pl.CostEstimate(
            flops=HEADS * BLOCK * BLOCK * HD * 8,
            bytes_accessed=5 * BLOCK * HEADS * HD,
            transcendentals=HEADS * BLOCK * BLOCK * 2,
        ),
        name="encode",
    )(meta, query, key, value, anchor)


def body(
    context_query,
    context_key,
    context_value,
    request_query,
    request_key,
    request_value,
    output_weight,
    block_lengths,
    query_host,
):
    pieces = Z * X
    chip = lax.axis_index("z") * X + lax.axis_index("x")
    host = chip * C + lax.axis_index("c")
    source = query_host[0]
    source_chip, source_core = source // C, source % C
    pair_lens = lax.dynamic_slice_in_dim(block_lengths, chip * C, C, 0)
    own_len = lax.dynamic_index_in_dim(block_lengths, host, 0, keepdims=False)
    meta = jnp.stack(
        [
            pair_lens[0],
            pair_lens[1],
            (chip == source_chip).astype(jnp.int32),
            source_core,
            own_len,
            jnp.where(host > 0, block_lengths[0], 0),
        ]
    )

    to_core, to_pair = pack(request_query, context_key, context_value, request_key, request_value, pieces)
    pair_rows = lax.all_gather(to_pair, "c", axis=0)
    from_core = lax.all_to_all(to_core, "c", 0, 0)
    to_chips = choose(source_core[None], from_core)
    from_chips = lax.all_to_all(to_chips, CHIPS, 0, 0, tiled=True)
    part = spread(source_chip[None], from_chips)
    queries = lax.all_to_all(part, CHIPS, 0, 0, tiled=True)
    anchor = lax.all_gather(queries[:, HALF * QUERY // pieces :, :].reshape(BLOCK, HD), "c", axis=0, tiled=True)

    sums = ask(meta, queries, pair_rows)
    met = lax.all_to_all(sums, CHIPS, 0, 0, tiled=True)
    merged = lax.all_to_all(merge(met), CHIPS, 0, 0, tiled=True)
    attended = lax.all_gather(merged.reshape(HALF * QUERY, HD), "c", axis=0, tiled=True)
    shares = project(attended, output_weight).reshape(-1, QUERY // lax.axis_size("head"), HD)
    shares = lax.all_to_all(shares, "head", 0, 0, tiled=True)
    request_output = jnp.sum(shares.astype(F32), axis=0).astype(BF16)

    encoded_context = encode(meta, context_query, context_key, context_value, anchor)
    return (encoded_context, request_output)


def solution(mesh):
    fine = Mesh(mesh.devices.reshape(Z, X, C, -1), ("z", "x", "c", "head"))
    ctx = ("z", "x", "c")
    placed = (P(ctx, "head"),) * 6 + (P("head", ctx), P(), P())
    return jax.shard_map(
        body,
        mesh=fine,
        in_specs=placed,
        out_specs=(P(ctx, "head"), P("head", ctx)),
        check_vma=False,
    )
```

time: 629 us -> 124 us (0.20)
  waiting for transfers between devices: 254 us -> 27.8 us
  blocking collectives: 257 us -> 31.3 us
  starting transfers between devices: 0.12 us -> 35.6 us
  matrix products: 35.1 us -> 0 us
  local copies, waits for them, and re-layouts: 32.1 us -> 6.5 us
  Pallas kernels: 0 us -> 19.4 us
  other arithmetic: 18.1 us -> 0.61 us
  between operations: 14.8 us -> 2.08 us
  loops' own time: 11 us -> 0 us
    psum x2 -> x0, waiting for transfers between devices: 222 us -> none  [the longest x1 199 us: broadcast(): return lax.psum(kept, axis)]
    psum x1 -> x0, blocking collectives: 130 us -> none  [body(): lax.psum((ask_values * rescale[:, :, None], ask_total * rescale), 'ctx')]
    pmax x1 -> x0, blocking collectives: 128 us -> none  [body(): global_peak = lax.pmax(ask_peak, 'ctx')]
    all_to_all x0 -> x5, starting transfers between devices: none -> 35.6 us  [the longest x1 10.4 us: body(): from_core = lax.all_to_all(to_core, 'c', 0, 0)]
    dot_general x33 -> x0, matrix products: 35.1 us -> none  [the longest x16 21.5 us: one_head(): lax.dot_general(query_head, key_rows, (((1,), (1,)), ((), ())), preferred...]
    reduce_scatter x1 -> x0, waiting for transfers between devices: 31.5 us -> none  [body(): lax.psum_scatter(jnp.dot(attended, output_weight, preferred_element_type=...]
    all_to_all x0 -> x5, waiting for transfers between devices: none -> 27.8 us  [the longest x1 13.9 us: body(): from_chips = lax.all_to_all(to_chips, CHIPS, 0, 0, tiled=True)]
    dynamic_update_slice x24 -> x0, local copies, waits for them, and re-layouts: 21.4 us -> none  [head_terms(): return lax.map(one_head, jnp.arange(local_heads, dtype=jnp.int32))]
  transfers between devices with their start and end apart: 3 -> 5, of which waited for: 3 -> 4; matrix products, arithmetic and copies ran while one was open for 7% -> 1% of each run, Pallas kernels for 0% -> 9%
where the time goes in v1:
time: 124 us; the launch traced here: 123 us
  starting transfers between devices  35.6 us (29%)
  blocking collectives  31.3 us (25%)
  waiting for transfers between devices  27.8 us (22%)
  Pallas kernels  19.4 us (16%)
  local copies, waits for them, and re-layouts  6.5 us (5%)
  between operations  2.08 us (2%)
    all_to_all x1, blocking collectives, body(): met = lax.all_to_all(sums, CHIPS, 0, 0, tiled=True)  18.1 us
    all_to_all x1, waiting for transfers between devices, body(): from_chips = lax.all_to_all(to_chips, CHIPS, 0, 0, tiled=True)  13.9 us
    pallas_call x1, Pallas kernels, encode(): pl.pallas_call(encode_kernel, out_shape=jax.ShapeDtypeStruct(query.shape,...  11.2 us
    all_to_all x1, starting transfers between devices, body(): from_core = lax.all_to_all(to_core, 'c', 0, 0)  10.4 us
    all_to_all x1, starting transfers between devices, body(): from_chips = lax.all_to_all(to_chips, CHIPS, 0, 0, tiled=True)  7.51 us
    all_to_all x1, starting transfers between devices, body(): shares = lax.all_to_all(shares, 'head', 0, 0, tiled=True)  6.95 us
    all_to_all x1, waiting for transfers between devices, body(): queries = lax.all_to_all(part, CHIPS, 0, 0, tiled=True)  6.58 us
    all_to_all x1, waiting for transfers between devices, body(): merged = lax.all_to_all(merge(met), CHIPS, 0, 0, tiled=True)  6.46 us
  transfers between devices with their start and end apart: 5, of which 4 were waited for; matrix products, arithmetic and copies ran while one was open for 1% of the time, Pallas kernels for 9%

profile of v1, /device:TPU:1, one launch (start us, length us, event | category | flops | bytes accessed | tf_op | source)
XLA Modules:
  0.0 123.3 jit_solution(15892508133634583580)
XLA Ops:
  0.6 0.0 copy-start
  0.6 1.0 copy-done
  1.7 0.0 copy-start.2
  1.7 0.9 copy-done.2
  2.6 0.0 copy-start.4
  2.6 0.9 copy-done.4
  3.5 0.0 copy-start.6
  3.5 0.8 copy-done.6
  4.3 0.0 copy-start.7
  4.3 0.8 copy-done.7
  5.2 1.0 pack.1
  6.2 10.4 %all-to-all-start = ((bf16[2,32,48,128]{3,2,1,0:T(8,128)(2,1)}), bf16[2,32,48,128]{3,2,1,0:T(8,128)(2,1)S(1)}, u32[]{:S(2)}, u32[]{:S(2)}) async-start(bf16[2,32,48,128]{3,2,1,0:T(8,128)(2,1)} %get-tuple-element.4), calls=%async_computation | async-start | bytes 1572864 | tf_op jit(solution)/shard_map/all_to_all | solution.py:335
  17.3 0.9 all-to-all-done.asked.anchor
  18.2 0.8 choose.1
  18.9 7.5 %all-to-all-start.1 = ((bf16[32,48,128]{2,1,0:T(8,128)(2,1)}), bf16[32,48,128]{2,1,0:T(8,128)(2,1)S(1)}, u32[]{:S(2)}, u32[]{:S(2)}) async-start(bf16[32,48,128]{2,1,0:T(8,128)(2,1)} %choose.1), calls=%async_computation.1 | async-start | bytes 786432 | tf_op jit(solution)/shard_map/all_to_all | solution.py:337
  26.5 13.9 %all-to-all-done.1.asked.anchor = bf16[32,48,128]{2,1,0:T(8,128)(2,1)S(1)} async-done(((bf16[32,48,128]{2,1,0:T(8,128)(2,1)}), bf16[32,48,128]{2,1,0:T(8,128)(2,1)S(1)}, u32[]{:S(2)}, u32[]{:S(2)}) %all-to-all-start.1) | async-done | bytes 393248 | tf_op jit(solution)/shard_map/all_to_all | solution.py:337
  40.3 0.8 spread.1
  41.1 5.0 %all-to-all-start.2 = ((bf16[32,48,128]{2,1,0:T(8,128)(2,1)}), bf16[32,48,128]{2,1,0:T(8,128)(2,1)S(1)}, u32[]{:S(2)}, u32[]{:S(2)}) async-start(bf16[32,48,128]{2,1,0:T(8,128)(2,1)} %spread.1), calls=%async_computation.2 | async-start | bytes 786432 | tf_op jit(solution)/shard_map/all_to_all | solution.py:339
  46.1 0.0 copy-start.9
  46.1 0.6 copy-done.9
  46.8 0.1 dynamic_slice.7
  46.9 0.6 fusion
  48.1 0.6 stack.20.meta
  48.7 3.7 %all-gather = bf16[3072,128]{1,0:T(8,128)(2,1)S(1)} all-gather(bf16[1536,128]{1,0:T(8,128)(2,1)S(1)} %get-tuple-element.5), channel_id=2, replica_groups=mesh['z'=8,'x'=4,'c'=2,'head'=8] {'c'}, dimensions={0}, use_global_device_ids=true | all-gather | bytes 1179648 | tf_op jit(solution)/shard_map/all_gather | solution.py:334
  52.4 6.6 %all-to-all-done.2.query = bf16[32,48,128]{2,1,0:T(8,128)(2,1)S(1)} async-done(((bf16[32,48,128]{2,1,0:T(8,128)(2,1)}), bf16[32,48,128]{2,1,0:T(8,128)(2,1)S(1)}, u32[]{:S(2)}, u32[]{:S(2)}) %all-to-all-start.2) | async-done | bytes 393248 | tf_op jit(solution)/shard_map/all_to_all | solution.py:339
  59.0 2.4 %ask.1 = bf16[32,48,128]{2,1,0:T(8,128)(2,1)S(1)} custom-call(s32[6]{0:T(128)S(1)} %stack.20.meta, bf16[32,48,128]{2,1,0:T(8,128)(2,1)S(1)} %all-to-all-done.2.query, bf16[2,1536,128]{2,1,0:T(8,128)(2,1)S(1)} %bitcast.14), custom_call_target="tpu_custom_call" | custom-call | tf_op jit(solution)/shard_map/ask/pallas_call | solution.py:192
  61.4 18.1 %all_to_all.30.received = bf16[32,48,128]{2,1,0:T(8,128)(2,1)S(1)} all-to-all(bf16[32,48,128]{2,1,0:T(8,128)(2,1)S(1)} %ask.1), channel_id=1, replica_groups=mesh['z'=8,'x'=4,'c'=2,'head'=8] {'z','x'}, dimensions={0} | all-to-all | bytes 786432 | tf_op jit(solution)/shard_map/all_to_all | solution.py:343
  79.5 2.2 %merge.1 = bf16[32,32,128]{2,1,0:T(8,128)(2,1)} custom-call(bf16[32,48,128]{2,1,0:T(8,128)(2,1)S(1)} %all_to_all.30.received), custom_call_target="tpu_custom_call" | custom-call | tf_op jit(solution)/shard_map/merge/pallas_call | solution.py:227
  81.7 5.8 %all-to-all-start.4 = ((bf16[32,32,128]{2,1,0:T(8,128)(2,1)}), bf16[32,32,128]{2,1,0:T(8,128)(2,1)S(1)}, u32[]{:S(2)}, u32[]{:S(2)}) async-start(bf16[32,32,128]{2,1,0:T(8,128)(2,1)} %merge.1), calls=%async_computation.4 | async-start | bytes 524288 | tf_op jit(solution)/shard_map/all_to_all | solution.py:344
  87.5 0.0 copy-start.8
  87.5 3.9 %all_gather.12.anchor = bf16[1024,128]{1,0:T(8,128)(2,1)S(1)} all-gather(bf16[512,128]{1,0:T(8,128)(2,1)S(1)} %bitcast.16), channel_id=1, replica_groups=mesh['z'=8,'x'=4,'c'=2,'head'=8] {'c'}, dimensions={0}, use_global_device_ids=true | all-gather | bytes 393216 | tf_op jit(solution)/shard_map/all_gather | solution.py:340
  91.4 6.5 %all-to-all-done.4 = bf16[32,32,128]{2,1,0:T(8,128)(2,1)S(1)} async-done(((bf16[32,32,128]{2,1,0:T(8,128)(2,1)}), bf16[32,32,128]{2,1,0:T(8,128)(2,1)S(1)}, u32[]{:S(2)}, u32[]{:S(2)}) %all-to-all-start.4) | async-done | bytes 262176 | tf_op jit(solution)/shard_map/all_to_all | solution.py:344
  97.9 0.0 copy-start.1
  97.9 5.7 %all_gather.15.attended = bf16[2048,128]{1,0:T(8,128)(2,1)S(1)} all-gather(bf16[1024,128]{1,0:T(8,128)(2,1)S(1)} %bitcast.15), channel_id=1, replica_groups=mesh['z'=8,'x'=4,'c'=2,'head'=8] {'c'}, dimensions={0}, use_global_device_ids=true | all-gather | bytes 786432 | tf_op jit(solution)/shard_map/all_gather | solution.py:345
  103.6 0.0 copy-done.1
  103.6 0.0 copy-start.5
  103.6 0.9 project.1
  104.5 0.0 copy-start.3
  104.5 7.0 %all-to-all-start.5 = ((bf16[8,32,128]{2,1,0:T(8,128)(2,1)}), bf16[8,32,128]{2,1,0:T(8,128)(2,1)S(1)}, u32[]{:S(2)}, u32[]{:S(2)}) async-start(bf16[8,32,128]{2,1,0:T(8,128)(2,1)} %bitcast.9), calls=%async_computation.5 | async-start | bytes 131072 | tf_op jit(solution)/shard_map/all_to_all | solution.py:347
  111.4 0.0 copy-done.8
  111.4 0.0 copy-done.5
  111.4 0.0 copy-done.3
  111.5 11.2 %encode.1 = bf16[512,1024]{1,0:T(8,128)(2,1)} custom-call(s32[6]{0:T(128)S(1)} %stack.20.meta, bf16[512,1024]{1,0:T(8,128)(2,1)S(1)} %copy-done.8, bf16[512,128]{1,0:T(8,128)(2,1)S(1)} %copy-done.3, bf16[512,128]{1,0:T(8,128)(2,1)S(1)} %copy-done.5, bf16[1024,128]{1,0:T(8,128)(2,1)S(1)} %all_gather.12.anchor), custom_call_target="tpu_custom_call" | custom-call | flops 2147483648 | bytes 2621440 | tf_op jit(solution)/shard_map/encode/pallas_call | solution.py:281
  122.7 0.0 all-to-all-done.5
  122.7 0.6 reduce_sum.12
  (1 shorter events, 0.0 us)
Async XLA Ops:
  0.6 1.0 copy-start
  1.7 0.9 copy-start.2
  2.6 0.9 copy-start.4
  3.5 0.8 copy-start.6
  4.3 0.8 copy-start.7
  6.2 12.0 %all-to-all-start = ((bf16[2,32,48,128]{3,2,1,0:T(8,128)(2,1)}), bf16[2,32,48,128]{3,2,1,0:T(8,128)(2,1)S(1)}, u32[]{:S(2)}, u32[]{:S(2)}) async-start(bf16[2,32,48,128]{3,2,1,0:T(8,128)(2,1)} %get-tuple-element.4), calls=%async_computation | async-start | bytes 1572864 | tf_op jit(solution)/shard_map/all_to_all | solution.py:335
  18.9 21.4 %all-to-all-start.1 = ((bf16[32,48,128]{2,1,0:T(8,128)(2,1)}), bf16[32,48,128]{2,1,0:T(8,128)(2,1)S(1)}, u32[]{:S(2)}, u32[]{:S(2)}) async-start(bf16[32,48,128]{2,1,0:T(8,128)(2,1)} %choose.1), calls=%async_computation.1 | async-start | bytes 786432 | tf_op jit(solution)/shard_map/all_to_all | solution.py:337
  41.1 17.8 %all-to-all-start.2 = ((bf16[32,48,128]{2,1,0:T(8,128)(2,1)}), bf16[32,48,128]{2,1,0:T(8,128)(2,1)S(1)}, u32[]{:S(2)}, u32[]{:S(2)}) async-start(bf16[32,48,128]{2,1,0:T(8,128)(2,1)} %spread.1), calls=%async_computation.2 | async-start | bytes 786432 | tf_op jit(solution)/shard_map/all_to_all | solution.py:339
  46.1 0.7 copy-start.9
  81.7 16.2 %all-to-all-start.4 = ((bf16[32,32,128]{2,1,0:T(8,128)(2,1)}), bf16[32,32,128]{2,1,0:T(8,128)(2,1)S(1)}, u32[]{:S(2)}, u32[]{:S(2)}) async-start(bf16[32,32,128]{2,1,0:T(8,128)(2,1)} %merge.1), calls=%async_computation.4 | async-start | bytes 524288 | tf_op jit(solution)/shard_map/all_to_all | solution.py:344
  87.5 24.0 %copy-start.8 = (bf16[512,1024]{1,0:T(8,128)(2,1)S(1)}, bf16[512,1024]{1,0:T(8,128)(2,1)}, u32[]{:S(2)}) copy-start(bf16[512,1024]{1,0:T(8,128)(2,1)} %query.3) | copy-start | bytes 3145732
  97.9 5.7 %copy-start.1 = (bf16[1024,128]{1,0:T(8,128)(2,1)S(1)}, bf16[1024,128]{1,0:T(8,128)(2,1)}, u32[]{:S(2)}) copy-start(bf16[1024,128]{1,0:T(8,128)(2,1)} %weight.1) | copy-start | bytes 786436
  103.6 7.9 %copy-start.5 = (bf16[512,128]{1,0:T(8,128)(2,1)S(1)}, bf16[512,128]{1,0:T(8,128)(2,1)}, u32[]{:S(2)}) copy-start(bf16[512,128]{1,0:T(8,128)(2,1)} %value.3) | copy-start | bytes 393220
  104.5 7.0 %copy-start.3 = (bf16[512,128]{1,0:T(8,128)(2,1)S(1)}, bf16[512,128]{1,0:T(8,128)(2,1)}, u32[]{:S(2)}) copy-start(bf16[512,128]{1,0:T(8,128)(2,1)} %key.3) | copy-start | bytes 393220
  104.5 18.2 %all-to-all-start.5 = ((bf16[8,32,128]{2,1,0:T(8,128)(2,1)}), bf16[8,32,128]{2,1,0:T(8,128)(2,1)S(1)}, u32[]{:S(2)}, u32[]{:S(2)}) async-start(bf16[8,32,128]{2,1,0:T(8,128)(2,1)} %bitcast.9), calls=%async_computation.5 | async-start | bytes 131072 | tf_op jit(solution)/shard_map/all_to_all | solution.py:347

commit v2 on v1

v2 whole, which is shorter than its diff:
```python
import jax
import jax.numpy as jnp
from jax import lax
from jax.experimental import pallas as pl
from jax.experimental.pallas import tpu as pltpu
from jax.sharding import Mesh, PartitionSpec as P

HD = 128
HEADS = 8
HALF = HEADS // 2
BLOCK = 512
QUERY = 256
Z, X, C = 8, 4, 2
SCALE = HD ** (-0.5) * 1.4426950408889634
NEG = -1e30
GROUPS = 4
BF16 = jnp.bfloat16
F32 = jnp.float32
CHIPS = ("z", "x")


def params(mib=32):
    return pltpu.CompilerParams(vmem_limit_bytes=mib * 1024 * 1024)


def smem():
    return pl.BlockSpec(memory_space=pltpu.SMEM)


def vmem():
    return pl.BlockSpec(memory_space=pltpu.VMEM)


def weigh(query, parts):
    scores = []
    for keys, _, seen in parts:
        score = lax.dot_general(query, keys, (((1,), (1,)), ((), ())), preferred_element_type=F32)
        scores.append(score if seen is None else jnp.where(seen, score, NEG))
    peak = scores[0].max(axis=1, keepdims=True)
    for score in scores[1:]:
        peak = jnp.maximum(peak, score.max(axis=1, keepdims=True))
    total = None
    for score, (_, values, _) in zip(scores, parts):
        weights = jnp.exp2((score - peak) * SCALE).astype(BF16)
        term = jnp.dot(weights, values, preferred_element_type=F32)
        total = term if total is None else total + term
    return peak, total[:, :HD], total[:, HD:]


def with_ones(values):
    return jnp.concatenate([values, jnp.ones(values.shape, BF16)], axis=1)


def column_ids(rows, cols):
    return lax.broadcasted_iota(jnp.int32, (rows, cols), 1)


def causal(size):
    return column_ids(size, size) <= lax.broadcasted_iota(jnp.int32, (size, size), 0)


def piece_rows():
    return QUERY // Z


def anchor_rows():
    return BLOCK // (Z * X)


def level_rows():
    return piece_rows() // GROUPS


def pack_kernel(host, query, key, value, send, keep):
    core = host[0] % C
    for out, half in ((send, 1 - core), (keep, core)):
        for head in range(HALF):
            column = pl.multiple_of((half * HALF + head) * HD, HD)
            out[:, head, : piece_rows(), :] = query[:, pl.ds(column, HD)].reshape(Z, piece_rows(), HD)

        @pl.when(half == 0)
        def _():
            out[:, :, piece_rows() :, :] = key[...].reshape(Z, X, anchor_rows(), HD)

        @pl.when(half == 1)
        def _():
            out[:, :, piece_rows() :, :] = value[...].reshape(Z, X, anchor_rows(), HD)


def pack(host, query, key, value):
    shape = (Z, X, piece_rows() + anchor_rows(), HD)
    return pl.pallas_call(
        pack_kernel,
        out_shape=(jax.ShapeDtypeStruct(shape, BF16),) * 2,
        grid=(1,),
        in_specs=[smem()] + [pl.BlockSpec(a.shape, lambda i: (0, 0)) for a in (query, key, value)],
        out_specs=(pl.BlockSpec(shape, lambda i: (0, 0, 0, 0)),) * 2,
        compiler_params=params(60),
        name="pack",
    )(host, query, key, value)


def join_kernel(*refs):
    out, row = refs[-1], 0
    for ref in refs[:-1]:
        out[row : row + ref.shape[0], :] = ref[...]
        row += ref.shape[0]


def join(*arrays):
    rows = sum(a.shape[0] for a in arrays)
    return pl.pallas_call(
        join_kernel,
        out_shape=jax.ShapeDtypeStruct((rows, HD), BF16),
        grid=(1,),
        in_specs=[pl.BlockSpec(a.shape, lambda i: (0, 0)) for a in arrays],
        out_specs=pl.BlockSpec((rows, HD), lambda i: (0, 0)),
        compiler_params=params(),
        name="join",
    )(*arrays)


def choose_kernel(host, source, kept, received, out):
    core = host[0] % C
    split = piece_rows()
    for part, mine in ((slice(0, split), source[0] % C == core), (slice(split, out.shape[2]), core == 0)):

        @pl.when(mine)
        def _():
            out[:, :, part, :] = kept[:, :, part, :]

        @pl.when(jnp.logical_not(mine))
        def _():
            out[:, :, part, :] = received[:, :, part, :]


def choose(host, source, kept, received):
    spec = pl.BlockSpec(kept.shape, lambda i: (0, 0, 0, 0))
    return pl.pallas_call(
        choose_kernel,
        out_shape=jax.ShapeDtypeStruct(kept.shape, BF16),
        grid=(1,),
        in_specs=[smem(), smem(), spec, spec],
        out_specs=spec,
        compiler_params=params(),
        name="choose",
    )(host, source, kept, received)


def spread_kernel(source, asked, anchor, out):
    split = piece_rows()
    out[:, :split, :] = jnp.broadcast_to(asked[:, :split, :], (out.shape[0], split, HD))
    out[:, split:, :] = jnp.broadcast_to(anchor[:, split:, :], (out.shape[0], out.shape[1] - split, HD))


def spread(source, received):
    pieces, rows, _ = received.shape
    return pl.pallas_call(
        spread_kernel,
        out_shape=jax.ShapeDtypeStruct(received.shape, BF16),
        grid_spec=pltpu.PrefetchScalarGridSpec(
            num_scalar_prefetch=1,
            grid=(1,),
            in_specs=[
                pl.BlockSpec((1, rows, HD), lambda i, source: (source[0] // C, 0, 0)),
                pl.BlockSpec((1, rows, HD), lambda i, source: (0, 0, 0)),
            ],
            out_specs=pl.BlockSpec(received.shape, lambda i, source: (0, 0, 0)),
        ),
        compiler_params=params(),
        name="spread",
    )(source, received, received)


def ask_kernel(host, source, lengths, query, rows, out, values):
    split = piece_rows()
    chip = host[0] // C
    for core in range(C):
        values[core] = with_ones(rows[core, BLOCK : 2 * BLOCK, :])

    def run(own):
        for head in range(HALF):
            asked = query[:, head, :split, :].reshape(QUERY, HD)
            parts = [
                (rows[core, :BLOCK, :], values[core], column_ids(QUERY, BLOCK) < lengths[chip * C + core])
                for core in range(C)
            ]
            if own:
                core = source[0] % C
                ask_key = rows[core, 2 * BLOCK : 2 * BLOCK + QUERY, :]
                ask_value = rows[core, 2 * BLOCK + QUERY :, :]
                parts.append((ask_key, with_ones(ask_value), causal(QUERY)))
            peak, numer, denom = weigh(asked, parts)
            out[:, head, :split, :] = (numer / denom).astype(BF16).reshape(Z, split, HD)
            level = peak * SCALE + jnp.log2(denom)
            high = level.astype(BF16).astype(F32)
            rest = level - high
            middle = rest.astype(BF16).astype(F32)
            lane = column_ids(QUERY, HD) % (HD // GROUPS)
            coded = jnp.where(lane == 0, high, jnp.where(lane == 1, middle, rest - middle))
            coded = coded.reshape(Z, GROUPS, level_rows(), HD)
            group = column_ids(level_rows(), HD) // (HD // GROUPS)
            side = coded[:, 0]
            for index in range(1, GROUPS):
                side = jnp.where((group == index)[None], coded[:, index], side)
            out[:, head, split:, :] = side.astype(BF16)

    here = source[0] // C == chip

    @pl.when(jnp.logical_not(here))
    def _():
        run(False)

    @pl.when(here)
    def _():
        run(True)


def ask(host, source, lengths, query, rows):
    return pl.pallas_call(
        ask_kernel,
        out_shape=jax.ShapeDtypeStruct((Z, X, piece_rows() + level_rows(), HD), BF16),
        in_specs=[smem()] * 3 + [vmem()] * 2,
        out_specs=vmem(),
        scratch_shapes=[pltpu.VMEM((C, BLOCK, 2 * HD), BF16)],
        compiler_params=params(),
        cost_estimate=pl.CostEstimate(
            flops=HALF * QUERY * C * BLOCK * HD * 6, bytes_accessed=1 << 20, transcendentals=HALF * QUERY * C * BLOCK
        ),
        name="ask",
    )(host, source, lengths, query, rows)


def merge_kernel(received, out):
    split, step = piece_rows(), level_rows()
    pieces = received.shape[0]
    lane = lax.broadcasted_iota(jnp.int32, (HD, GROUPS * HD), 0)
    column = lax.broadcasted_iota(jnp.int32, (HD, GROUPS * HD), 1)
    width = HD // GROUPS
    adder = ((lane // width == column // HD) & (lane % width < 3)).astype(F32).astype(BF16)
    coded = received[:, split:, :].reshape(pieces * step, HD)
    levels = jnp.dot(coded, adder, preferred_element_type=F32).reshape(pieces, step, GROUPS * HD)
    for group in range(GROUPS):
        level = levels[:, :, group * HD : (group + 1) * HD]
        share = jnp.exp2(level - level.max(axis=0, keepdims=True))
        rows = slice(group * step, (group + 1) * step)
        numer = jnp.sum(share * received[:, rows, :].astype(F32), axis=0)
        merged = (numer / jnp.sum(share, axis=0)).astype(BF16)
        out[:, rows, :] = jnp.broadcast_to(merged[None], (pieces, step, HD))


def merge(received):
    return pl.pallas_call(
        merge_kernel,
        out_shape=jax.ShapeDtypeStruct((received.shape[0], piece_rows(), HD), BF16),
        in_specs=[vmem()],
        out_specs=vmem(),
        compiler_params=params(),
        name="merge",
    )(received)


def project_kernel(host, attended, weight, other, out):
    core = host[0] % C
    rows = [
        jnp.concatenate([attended[z, x] for x in range(X)], axis=1) for z in range(Z)
    ]
    rows = jnp.concatenate(rows, axis=0)
    first = pl.multiple_of(core * HALF * HD, HALF * HD)
    mine = jnp.dot(rows, weight[pl.ds(first, HALF * HD), :], preferred_element_type=F32)
    others = jnp.dot(rows, other[...], preferred_element_type=F32)
    out[pl.ds(core, 1)] = mine.astype(BF16)[None]
    out[pl.ds(1 - core, 1)] = others.astype(BF16)[None]


def project(host, attended, weight, other):
    return pl.pallas_call(
        project_kernel,
        out_shape=jax.ShapeDtypeStruct((C, QUERY, HD), BF16),
        in_specs=[smem()] + [vmem()] * 3,
        out_specs=vmem(),
        compiler_params=params(),
        name="project",
    )(host, attended, weight, other)


def total_kernel(shares, out):
    out[...] = jnp.sum(shares[...].astype(F32), axis=0).astype(BF16)


def total(shares):
    return pl.pallas_call(
        total_kernel,
        out_shape=jax.ShapeDtypeStruct(shares.shape[1:], BF16),
        in_specs=[vmem()],
        out_specs=vmem(),
        compiler_params=params(),
        name="total",
    )(shares)


def encode_kernel(host, lengths, query, key, value, anchor, *rest):
    out, own_values, anchor_values = rest[-3:]

    @pl.when(pl.program_id(0) == 0)
    def _():
        own_values[...] = with_ones(value[...])
        anchor_values[...] = with_ones(anchor[BLOCK:, :])

    own_len = lengths[host[0]]
    anchor_len = jnp.where(host[0] > 0, lengths[0], 0)
    half = BLOCK // 2
    for tile in range(2):
        rows = slice(tile * half, (tile + 1) * half)
        parts = [
            (key[rows, :], own_values[rows, :], causal(half)),
            (anchor[:BLOCK, :], anchor_values[...], column_ids(half, BLOCK) < anchor_len),
        ]
        if tile:
            parts.append((key[:half, :], own_values[:half, :], None))
        _, numer, denom = weigh(query[rows, :], parts)
        live = lax.broadcasted_iota(jnp.int32, (half, HD), 0) + tile * half < own_len
        out[rows, :] = jnp.where(live, numer / denom, 0.0).astype(BF16)


def encode(host, lengths, query, key, value, anchor, first, count, done=None):
    whole = pl.BlockSpec((BLOCK, HD), lambda h: (0, 0))
    heads = pl.BlockSpec((BLOCK, HD), lambda h: (0, h + first))
    given = () if done is None else (done,)
    return pl.pallas_call(
        encode_kernel,
        out_shape=jax.ShapeDtypeStruct(query.shape, BF16),
        grid=(count,),
        in_specs=[smem(), smem(), heads, whole, whole, pl.BlockSpec((2 * BLOCK, HD), lambda h: (0, 0))]
        + [pl.BlockSpec(memory_space=pl.ANY)] * len(given),
        out_specs=heads,
        scratch_shapes=[pltpu.VMEM((BLOCK, 2 * HD), BF16)] * 2,
        input_output_aliases={6: 0} if given else {},
        compiler_params=params(),
        cost_estimate=pl.CostEstimate(
            flops=count * BLOCK * BLOCK * HD * 10,
            bytes_accessed=5 * BLOCK * count * HD,
            transcendentals=count * BLOCK * BLOCK * 2,
        ),
        name="encode",
    )(host, lengths, query, key, value, anchor, *given)


def body(
    context_query,
    context_key,
    context_value,
    request_query,
    request_key,
    request_value,
    output_weight,
    block_lengths,
    query_host,
):
    pieces = Z * X
    core = lax.axis_index("c")
    host = lax.axis_index(("z", "x", "c")).astype(jnp.int32)[None]

    send, keep = pack(host, request_query, context_key, context_value)
    came = lax.ppermute(send, "c", [(0, 1), (1, 0)])
    to_chips = choose(host, query_host, keep, came).reshape(pieces, -1, HD)
    from_chips = lax.all_to_all(to_chips, CHIPS, 0, 0, tiled=True)
    pair_rows = lax.all_gather(join(context_key, context_value, request_key, request_value), "c", axis=0)
    weight_half = lax.dynamic_slice_in_dim(output_weight, (1 - core) * HALF * HD, HALF * HD, 0)
    other_weight = lax.ppermute(weight_half, "c", [(0, 1), (1, 0)])
    from_chips, pair_rows, other_weight = lax.optimization_barrier((from_chips, pair_rows, other_weight))
    part = spread(query_host, from_chips)
    queries = lax.all_to_all(part, CHIPS, 0, 0, tiled=True)

    sums = ask(host, query_host, block_lengths, queries.reshape(Z, X, -1, HD), pair_rows)
    met = lax.all_to_all(sums.reshape(pieces, -1, HD), CHIPS, 0, 0, tiled=True)
    anchor = lax.all_gather(queries[:, piece_rows() :, :].reshape(BLOCK, HD), "c", axis=0, tiled=True)
    context = (host, block_lengths, context_query, context_key, context_value, anchor)
    encoded = encode(*context, 0, HEADS // 2)
    met, encoded = lax.optimization_barrier((met, encoded))
    gathered = lax.all_to_all(merge(met), CHIPS, 0, 0, tiled=True)
    encoded_context = encode(*context, HEADS // 2, HEADS // 2, encoded)
    gathered, encoded_context = lax.optimization_barrier((gathered, encoded_context))
    shares = project(host, gathered.reshape(Z, X, -1, HD), output_weight, other_weight)
    blocks = lax.axis_size("head")
    shares = lax.all_to_all(shares.reshape(C * blocks, -1, HD), ("c", "head"), 0, 0, tiled=True)
    return (encoded_context, total(shares))


def solution(mesh):
    fine = Mesh(mesh.devices.reshape(Z, X, C, -1), ("z", "x", "c", "head"))
    ctx = ("z", "x", "c")
    placed = (P(ctx, "head"),) * 6 + (P("head", ctx), P(), P())
    return jax.shard_map(
        body,
        mesh=fine,
        in_specs=placed,
        out_specs=(P(ctx, "head"), P("head", ctx)),
        check_vma=False,
    )
```

time: 124 us -> 114 us (0.919)
  waiting for transfers between devices: 27.8 us -> 15.8 us
  blocking collectives: 31.3 us -> 40.1 us
  local copies, waits for them, and re-layouts: 6.5 us -> 1.7 us
  starting transfers between devices: 35.6 us -> 33.5 us
    all_to_all x1 -> x2, blocking collectives: 18.1 us -> 34.1 us  [the longest x1 17.6 us: body(): queries = lax.all_to_all(part, CHIPS, 0, 0, tiled=True)]
    all_to_all x4 -> x2, starting transfers between devices: 28.1 us -> 14.4 us  [the longest x1 8.63 us: body(): gathered = lax.all_to_all(merge(met), CHIPS, 0, 0, tiled=True)]
    ppermute x0 -> x2, starting transfers between devices: none -> 11.5 us  [the longest x1 8.77 us: body(): came = lax.ppermute(send, 'c', [(0, 1), (1, 0)])]
    all_to_all x4 -> x2, waiting for transfers between devices: 13.9 us -> 6.24 us  [the longest x1 5.36 us: body(): gathered = lax.all_to_all(merge(met), CHIPS, 0, 0, tiled=True)]
    all_gather x3 -> x2, blocking collectives: 13.3 us -> 6.01 us  [the longest x1 3.64 us: body(): lax.all_gather(queries[:, piece_rows():, :].reshape(BLOCK, HD), 'c', axis...]
    all_to_all x1, waiting for transfers between devices: 13.9 us -> 8.66 us  [body(): from_chips = lax.all_to_all(to_chips, CHIPS, 0, 0, tiled=True)]
    unnamed x20 -> x16, local copies, waits for them, and re-layouts: 5.19 us -> 1.68 us
    pallas_call x1 -> x2, Pallas kernels: 11.2 us -> 12.4 us  [encode(): pl.pallas_call(encode_kernel, out_shape=jax.ShapeDtypeStruct(query.shape,...]
  transfers between devices with their start and end apart: 5 -> 5, of which waited for: 4 -> 4; matrix products, arithmetic and copies ran while one was open for 1% -> 0% of each run, Pallas kernels for 9% -> 11%
where the time goes in v2:
time: 114 us; the launch traced here: 113 us
  blocking collectives  40.1 us (35%)
  starting transfers between devices  33.5 us (29%)
  Pallas kernels  20.6 us (18%)
  waiting for transfers between devices  15.8 us (14%)
  local copies, waits for them, and re-layouts  1.7 us (1%)
  between operations  1.43 us (1%)
    all_to_all x1, blocking collectives, body(): queries = lax.all_to_all(part, CHIPS, 0, 0, tiled=True)  17.6 us
    all_to_all x1, blocking collectives, body(): lax.all_to_all(shares.reshape(C * blocks, -1, HD), ('c', 'head'), 0, 0, t...  16.5 us
    pallas_call x2, Pallas kernels, encode(): pl.pallas_call(encode_kernel, out_shape=jax.ShapeDtypeStruct(query.shape,...  12.4 us
    ppermute x1, starting transfers between devices, body(): came = lax.ppermute(send, 'c', [(0, 1), (1, 0)])  8.77 us
    all_to_all x1, waiting for transfers between devices, body(): from_chips = lax.all_to_all(to_chips, CHIPS, 0, 0, tiled=True)  8.66 us
    all_to_all x1, starting transfers between devices, body(): gathered = lax.all_to_all(merge(met), CHIPS, 0, 0, tiled=True)  8.63 us
    all_to_all x1, starting transfers between devices, body(): from_chips = lax.all_to_all(to_chips, CHIPS, 0, 0, tiled=True)  7.65 us
    all_to_all x1, starting transfers between devices, body(): met = lax.all_to_all(sums.reshape(pieces, -1, HD), CHIPS, 0, 0, tiled=True)  5.8 us
  transfers between devices with their start and end apart: 5, of which 4 were waited for; matrix products, arithmetic and copies ran while one was open for 0% of the time, Pallas kernels for 11%

profile of v2, /device:TPU:1, one launch (start us, length us, event | category | flops | bytes accessed | tf_op | source)
XLA Modules:
  0.0 113.2 jit_solution(12273685058050630045)
XLA Ops:
  0.6 2.2 %pack.1 = (bf16[8,4,48,128]{3,2,1,0:T(8,128)(2,1)}, bf16[8,4,48,128]{3,2,1,0:T(8,128)(2,1)}) custom-call(s32[1]{0:T(128)} %bitcast.host, bf16[256,1024]{1,0:T(8,128)(2,1)} %query.3, bf16[512,128]{1,0:T(8,128)(2,1)} %key.5, bf16[512,128]{1,0:T(8,128)(2,1)} %value.5), custom_call_target="tpu_custom_call" | custom-call | tf_op jit(solution)/shard_map/pack/pallas_call | solution.py:92
  2.8 8.8 %collective-permute-start = (bf16[8,4,48,128]{3,2,1,0:T(8,128)(2,1)}, bf16[8,4,48,128]{3,2,1,0:T(8,128)(2,1)S(1)}, u32[]{:S(2)}, u32[]{:S(2)}) collective-permute-start(bf16[8,4,48,128]{3,2,1,0:T(8,128)(2,1)} %get-tuple-element.12), channel_id=1, source_target_pairs={{0,8},{8,0},{1,9},{9,1},{2,10},{10,2},{3,11},{11,3},{4,12},{12,4},... | collective-permute-start | bytes 1179656 | tf_op jit(solution)/shard_map/ppermute | solution.py:365
  12.2 0.9 collective-permute-done.received
  13.1 0.0 copy-start.3
  13.1 1.0 copy-done.3
  14.1 0.8 choose.1
  14.9 0.0 copy-start
  14.9 0.0 copy-start.4
  14.9 0.0 copy-start.5
  14.9 7.6 %all-to-all-start = ((bf16[32,48,128]{2,1,0:T(8,128)(2,1)}), bf16[32,48,128]{2,1,0:T(8,128)(2,1)S(1)}, u32[]{:S(2)}, u32[]{:S(2)}) async-start(bf16[32,48,128]{2,1,0:T(8,128)(2,1)} %bitcast.1), calls=%async_computation | async-start | bytes 786432 | tf_op jit(solution)/shard_map/all_to_all | solution.py:367
  22.6 0.0 copy-done
  22.6 0.0 copy-start.1
  22.6 0.0 copy-start.2
  22.6 2.7 %collective-permute-start.1 = (bf16[512,128]{1,0:T(8,128)(2,1)S(1)}, bf16[512,128]{1,0:T(8,128)(2,1)S(1)}, u32[]{:S(2)}, u32[]{:S(2)}) collective-permute-start(bf16[512,128]{1,0:T(8,128)(2,1)S(1)} %constant_dynamic-slice_fusion), channel_id=1, source_target_pairs={{0,8},{8,0},{1,9},{9,1},{2,10},{10,2},{3,11},{11,3},{4,12},{12,4},... | collective-permute-start | bytes 393224 | tf_op jit(solution)/shard_map/ppermute | solution.py:370
  25.3 0.0 copy-done.4
  25.3 0.0 copy-done.5
  25.4 0.0 copy-done.1
  25.4 0.0 copy-done.2
  25.4 2.4 %all-gather = bf16[3072,128]{1,0:T(8,128)(2,1)S(1)} all-gather(bf16[1536,128]{1,0:T(8,128)(2,1)S(1)} %join.1), channel_id=2, replica_groups=mesh['z'=8,'x'=4,'c'=2,'head'=8] {'c'}, dimensions={0}, use_global_device_ids=true | all-gather | bytes 1179648 | tf_op jit(solution)/shard_map/all_gather | solution.py:368
  27.8 0.0 collective-permute-done.1.other
  27.8 8.7 %all-to-all-done.asked.anchor = bf16[32,48,128]{2,1,0:T(8,128)(2,1)S(1)} async-done(((bf16[32,48,128]{2,1,0:T(8,128)(2,1)}), bf16[32,48,128]{2,1,0:T(8,128)(2,1)S(1)}, u32[]{:S(2)}, u32[]{:S(2)}) %all-to-all-start) | async-done | bytes 393248 | tf_op jit(solution)/shard_map/all_to_all | solution.py:367
  36.4 0.1 spread.1
  36.5 17.6 %all_to_all.25 = bf16[32,48,128]{2,1,0:T(8,128)(2,1)S(1)} all-to-all(bf16[32,48,128]{2,1,0:T(8,128)(2,1)S(1)} %spread.1), channel_id=1, replica_groups=mesh['z'=8,'x'=4,'c'=2,'head'=8] {'z','x'}, dimensions={0} | all-to-all | bytes 786432 | tf_op jit(solution)/shard_map/all_to_all | solution.py:373
  54.1 0.0 copy-start.7
  54.1 0.7 copy-done.7
  54.8 3.2 %ask.1 = bf16[8,4,40,128]{3,2,1,0:T(8,128)(2,1)} custom-call(s32[1]{0:T(128)} %bitcast.host, s32[1]{0:T(128)S(6)} %copy.13.source, s32[64]{0:T(128)S(1)} %copy-done.7, bf16[8,4,48,128]{3,2,1,0:T(8,128)(2,1)S(1)} %bitcast.10, bf16[2,1536,128]{2,1,0:T(8,128)(2,1)S(1)} %bitcast.9), custom_call_target="tpu_custom_call" | custom-call | flops 805306368 | bytes 1048576 | tf_op jit(solution)/shard_map/ask/pallas_call | solution.py:220
  57.9 0.0 copy-start.6
  57.9 5.8 %all-to-all-start.2 = ((bf16[32,40,128]{2,1,0:T(8,128)(2,1)}), bf16[32,40,128]{2,1,0:T(8,128)(2,1)S(1)}, u32[]{:S(2)}, u32[]{:S(2)}) async-start(bf16[32,40,128]{2,1,0:T(8,128)(2,1)} %bitcast.4), calls=%async_computation.2 | async-start | bytes 655360 | tf_op jit(solution)/shard_map/all_to_all | solution.py:376
  63.8 3.6 %all_gather.11.anchor = bf16[1024,128]{1,0:T(8,128)(2,1)S(1)} all-gather(bf16[512,128]{1,0:T(8,128)(2,1)S(1)} %bitcast.12), channel_id=1, replica_groups=mesh['z'=8,'x'=4,'c'=2,'head'=8] {'c'}, dimensions={0}, use_global_device_ids=true | all-gather | bytes 393216 | tf_op jit(solution)/shard_map/all_gather | solution.py:377
  67.4 0.0 copy-done.6
  67.4 6.2 %encode.2.rest_0_ = bf16[512,1024]{1,0:T(8,128)(2,1)} custom-call(s32[1]{0:T(128)} %bitcast.host, s32[64]{0:T(128)S(1)} %copy-done.7, bf16[512,1024]{1,0:T(8,128)(2,1)S(1)} %copy-done.6, bf16[512,128]{1,0:T(8,128)(2,1)S(1)} %copy-done.1, bf16[512,128]{1,0:T(8,128)(2,1)S(1)} %copy-done.2, bf16[1024,128]{1,0:T(8,128)(2,1)S(1)} %all_gather.11.anchor), custom_call_target="tpu_custom_call" | custom-call | flops 1342177280 | bytes 1310720 | tf_op jit(solution)/shard_map/encode/pallas_call | solution.py:330
  73.6 0.9 all-to-all-done.2.received
  74.5 1.1 merge.1
  75.5 8.6 %all-to-all-start.3 = ((bf16[32,32,128]{2,1,0:T(8,128)(2,1)}), bf16[32,32,128]{2,1,0:T(8,128)(2,1)S(1)}, u32[]{:S(2)}, u32[]{:S(2)}) async-start(bf16[32,32,128]{2,1,0:T(8,128)(2,1)} %merge.1), calls=%async_computation.3 | async-start | bytes 524288 | tf_op jit(solution)/shard_map/all_to_all | solution.py:381
  84.2 6.2 %encode.3 = bf16[512,1024]{1,0:T(8,128)(2,1)} custom-call(s32[1]{0:T(128)} %bitcast.host, s32[64]{0:T(128)S(1)} %copy-done.7, bf16[512,1024]{1,0:T(8,128)(2,1)S(1)} %copy-done.6, bf16[512,128]{1,0:T(8,128)(2,1)S(1)} %copy-done.1, bf16[512,128]{1,0:T(8,128)(2,1)S(1)} %copy-done.2, ...), custom_call_target="tpu_custom_call", output_to_operand_aliasing={{}: (6, {})} | custom-call | flops 1342177280 | bytes 1310720 | tf_op jit(solution)/shard_map/encode/pallas_call | solution.py:330
  90.4 5.4 %all-to-all-done.3 = bf16[32,32,128]{2,1,0:T(8,128)(2,1)S(1)} async-done(((bf16[32,32,128]{2,1,0:T(8,128)(2,1)}), bf16[32,32,128]{2,1,0:T(8,128)(2,1)S(1)}, u32[]{:S(2)}, u32[]{:S(2)}) %all-to-all-start.3) | async-done | bytes 262176 | tf_op jit(solution)/shard_map/all_to_all | solution.py:381
  95.8 0.3 project.1
  96.1 16.5 %all_to_all.26.shares = bf16[16,32,128]{2,1,0:T(8,128)(2,1)S(1)} all-to-all(bf16[16,32,128]{2,1,0:T(8,128)(2,1)S(1)} %bitcast.11), channel_id=1, replica_groups=mesh['z'=8,'x'=4,'c'=2,'head'=8] {'c','head'}, dimensions={0} | all-to-all | bytes 262144 | tf_op jit(solution)/shard_map/all_to_all | solution.py:386
  112.6 0.6 total.1
  (3 shorter events, 0.1 us)
Async XLA Ops:
  2.8 10.3 %collective-permute-start = (bf16[8,4,48,128]{3,2,1,0:T(8,128)(2,1)}, bf16[8,4,48,128]{3,2,1,0:T(8,128)(2,1)S(1)}, u32[]{:S(2)}, u32[]{:S(2)}) collective-permute-start(bf16[8,4,48,128]{3,2,1,0:T(8,128)(2,1)} %get-tuple-element.12), channel_id=1, source_target_pairs={{0,8},{8,0},{1,9},{9,1},{2,10},{10,2},{3,11},{11,3},{4,12},{12,4},... | collective-permute-start | bytes 1179656 | tf_op jit(solution)/shard_map/ppermute | solution.py:365
  13.1 1.0 copy-start.3
  14.9 7.7 %copy-start = (bf16[1024,128]{1,0:T(8,128)(2,1)S(1)}, bf16[1024,128]{1,0:T(8,128)(2,1)}, u32[]{:S(2)}) copy-start(bf16[1024,128]{1,0:T(8,128)(2,1)} %weight.1) | copy-start | bytes 786436
  14.9 10.4 %copy-start.4 = (bf16[256,128]{1,0:T(8,128)(2,1)S(1)}, bf16[256,128]{1,0:T(8,128)(2,1)}, u32[]{:S(2)}) copy-start(bf16[256,128]{1,0:T(8,128)(2,1)} %refs_2_.1) | copy-start | bytes 196612
  14.9 10.4 %copy-start.5 = (bf16[256,128]{1,0:T(8,128)(2,1)S(1)}, bf16[256,128]{1,0:T(8,128)(2,1)}, u32[]{:S(2)}) copy-start(bf16[256,128]{1,0:T(8,128)(2,1)} %refs_3_.1) | copy-start | bytes 196612
  14.9 21.5 %all-to-all-start = ((bf16[32,48,128]{2,1,0:T(8,128)(2,1)}), bf16[32,48,128]{2,1,0:T(8,128)(2,1)S(1)}, u32[]{:S(2)}, u32[]{:S(2)}) async-start(bf16[32,48,128]{2,1,0:T(8,128)(2,1)} %bitcast.1), calls=%async_computation | async-start | bytes 786432 | tf_op jit(solution)/shard_map/all_to_all | solution.py:367
  22.6 2.8 %copy-start.1 = (bf16[512,128]{1,0:T(8,128)(2,1)S(1)}, bf16[512,128]{1,0:T(8,128)(2,1)}, u32[]{:S(2)}) copy-start(bf16[512,128]{1,0:T(8,128)(2,1)} %key.5) | copy-start | bytes 393220
  22.6 2.8 %copy-start.2 = (bf16[512,128]{1,0:T(8,128)(2,1)S(1)}, bf16[512,128]{1,0:T(8,128)(2,1)}, u32[]{:S(2)}) copy-start(bf16[512,128]{1,0:T(8,128)(2,1)} %value.5) | copy-start | bytes 393220
  22.6 5.2 %collective-permute-start.1 = (bf16[512,128]{1,0:T(8,128)(2,1)S(1)}, bf16[512,128]{1,0:T(8,128)(2,1)S(1)}, u32[]{:S(2)}, u32[]{:S(2)}) collective-permute-start(bf16[512,128]{1,0:T(8,128)(2,1)S(1)} %constant_dynamic-slice_fusion), channel_id=1, source_target_pairs={{0,8},{8,0},{1,9},{9,1},{2,10},{10,2},{3,11},{11,3},{4,12},{12,4},... | collective-permute-start | bytes 393224 | tf_op jit(solution)/shard_map/ppermute | solution.py:370
  54.1 0.7 copy-start.7
  57.9 9.5 %copy-start.6 = (bf16[512,1024]{1,0:T(8,128)(2,1)S(1)}, bf16[512,1024]{1,0:T(8,128)(2,1)}, u32[]{:S(2)}) copy-start(bf16[512,1024]{1,0:T(8,128)(2,1)} %query.5) | copy-start | bytes 3145732
  57.9 16.6 %all-to-all-start.2 = ((bf16[32,40,128]{2,1,0:T(8,128)(2,1)}), bf16[32,40,128]{2,1,0:T(8,128)(2,1)S(1)}, u32[]{:S(2)}, u32[]{:S(2)}) async-start(bf16[32,40,128]{2,1,0:T(8,128)(2,1)} %bitcast.4), calls=%async_computation.2 | async-start | bytes 655360 | tf_op jit(solution)/shard_map/all_to_all | solution.py:376
  75.5 20.2 %all-to-all-start.3 = ((bf16[32,32,128]{2,1,0:T(8,128)(2,1)}), bf16[32,32,128]{2,1,0:T(8,128)(2,1)S(1)}, u32[]{:S(2)}, u32[]{:S(2)}) async-start(bf16[32,32,128]{2,1,0:T(8,128)(2,1)} %merge.1), calls=%async_computation.3 | async-start | bytes 524288 | tf_op jit(solution)/shard_map/all_to_all | solution.py:381

commit v3 on v2

--- a/solution.py
+++ b/solution.py
@@ -71,33 +71,57 @@
     return piece_rows() // GROUPS
 
 
-def pack_kernel(host, query, key, value, send, keep):
+def pack_kernel(host, source, query, came, *rest):
+    anchors, out = rest[:-1], rest[-1]
     core = host[0] % C
-    for out, half in ((send, 1 - core), (keep, core)):
+    first = pl.multiple_of(core * HALF * HD, HALF * HD)
+
+    def put(rows):
         for head in range(HALF):
-            column = pl.multiple_of((half * HALF + head) * HD, HD)
-            out[:, head, : piece_rows(), :] = query[:, pl.ds(column, HD)].reshape(Z, piece_rows(), HD)
-
-        @pl.when(half == 0)
+            out[:, head, : piece_rows(), :] = rows[:, pl.ds(first + head * HD, HD)].reshape(Z, piece_rows(), HD)
+
+    here = source[0] % C == core
+
+    @pl.when(here)
+    def _():
+        put(query)
+
+    @pl.when(jnp.logical_not(here))
+    def _():
+        put(came)
+
+    for index, rows in enumerate(anchors):
+
+        @pl.when(core == index)
         def _():
-            out[:, :, piece_rows() :, :] = key[...].reshape(Z, X, anchor_rows(), HD)
-
-        @pl.when(half == 1)
-        def _():
-            out[:, :, piece_rows() :, :] = value[...].reshape(Z, X, anchor_rows(), HD)
-
-
-def pack(host, query, key, value):
+            out[:, :, piece_rows() :, :] = rows[...].reshape(Z, X, anchor_rows(), HD)
+
+
+def pack(host, source, *arrays):
     shape = (Z, X, piece_rows() + anchor_rows(), HD)
     return pl.pallas_call(
         pack_kernel,
-        out_shape=(jax.ShapeDtypeStruct(shape, BF16),) * 2,
-        grid=(1,),
-        in_specs=[smem()] + [pl.BlockSpec(a.shape, lambda i: (0, 0)) for a in (query, key, value)],
-        out_specs=(pl.BlockSpec(shape, lambda i: (0, 0, 0, 0)),) * 2,
-        compiler_params=params(60),
+        out_shape=jax.ShapeDtypeStruct(shape, BF16),
+        in_specs=[smem()] * 2 + [vmem()] * len(arrays),
+        out_specs=vmem(),
+        compiler_params=params(),
         name="pack",
-    )(host, query, key, value)
+    )(host, source, *arrays)
+
+
+def blank_kernel(out):
+    pass
+
+
+def blank():
+    shape = (Z, X, piece_rows() + anchor_rows(), HD)
+    return pl.pallas_call(
+        blank_kernel, out_shape=jax.ShapeDtypeStruct(shape, BF16), out_specs=anywhere(), name="blank"
+    )()
+
+
+def anywhere():
+    return pl.BlockSpec(memory_space=pl.ANY)
 
 
 def join_kernel(*refs):
@@ -118,33 +142,6 @@
         compiler_params=params(),
         name="join",
     )(*arrays)
-
-
-def choose_kernel(host, source, kept, received, out):
-    core = host[0] % C
-    split = piece_rows()
-    for part, mine in ((slice(0, split), source[0] % C == core), (slice(split, out.shape[2]), core == 0)):
-
-        @pl.when(mine)
-        def _():
-            out[:, :, part, :] = kept[:, :, part, :]
-
-        @pl.when(jnp.logical_not(mine))
-        def _():
-            out[:, :, part, :] = received[:, :, part, :]
-
-
-def choose(host, source, kept, received):
-    spec = pl.BlockSpec(kept.shape, lambda i: (0, 0, 0, 0))
-    return pl.pallas_call(
-        choose_kernel,
-        out_shape=jax.ShapeDtypeStruct(kept.shape, BF16),
-        grid=(1,),
-        in_specs=[smem(), smem(), spec, spec],
-        out_specs=spec,
-        compiler_params=params(),
-        name="choose",
-    )(host, source, kept, received)
 
 
 def spread_kernel(source, asked, anchor, out):
@@ -172,7 +169,16 @@
     )(source, received, received)
 
 
-def ask_kernel(host, source, lengths, query, rows, out, values):
+def sideways(rows):
+    rows = rows.reshape(Z, GROUPS, level_rows(), HD)
+    group = column_ids(level_rows(), HD)[None] // (HD // GROUPS)
+    side = rows[:, 0]
+    for index in range(1, GROUPS):
+        side = jnp.where(group == index, rows[:, index], side)
+    return side
+
+
+def ask_kernel(host, source, meta, query, rows, out, values):
     split = piece_rows()
     chip = host[0] // C
     for core in range(C):
@@ -182,7 +188,7 @@
         for head in range(HALF):
             asked = query[:, head, :split, :].reshape(QUERY, HD)
             parts = [
-                (rows[core, :BLOCK, :], values[core], column_ids(QUERY, BLOCK) < lengths[chip * C + core])
+                (rows[core, :BLOCK, :], values[core], column_ids(QUERY, BLOCK) < meta[core])
                 for core in range(C)
             ]
             if own:
@@ -192,18 +198,13 @@
                 parts.append((ask_key, with_ones(ask_value), causal(QUERY)))
             peak, numer, denom = weigh(asked, parts)
             out[:, head, :split, :] = (numer / denom).astype(BF16).reshape(Z, split, HD)
-            level = peak * SCALE + jnp.log2(denom)
-            high = level.astype(BF16).astype(F32)
-            rest = level - high
+            side = sideways(jnp.broadcast_to(peak, denom.shape)) * SCALE + jnp.log2(sideways(denom))
+            high = side.astype(BF16).astype(F32)
+            rest = side - high
             middle = rest.astype(BF16).astype(F32)
-            lane = column_ids(QUERY, HD) % (HD // GROUPS)
+            lane = column_ids(level_rows(), HD)[None] % (HD // GROUPS)
             coded = jnp.where(lane == 0, high, jnp.where(lane == 1, middle, rest - middle))
-            coded = coded.reshape(Z, GROUPS, level_rows(), HD)
-            group = column_ids(level_rows(), HD) // (HD // GROUPS)
-            side = coded[:, 0]
-            for index in range(1, GROUPS):
-                side = jnp.where((group == index)[None], coded[:, index], side)
-            out[:, head, split:, :] = side.astype(BF16)
+            out[:, head, split:, :] = coded.astype(BF16)
 
     here = source[0] // C == chip
 
@@ -216,7 +217,7 @@
         run(True)
 
 
-def ask(host, source, lengths, query, rows):
+def ask(host, source, meta, query, rows):
     return pl.pallas_call(
         ask_kernel,
         out_shape=jax.ShapeDtypeStruct((Z, X, piece_rows() + level_rows(), HD), BF16),
@@ -228,7 +229,7 @@
             flops=HALF * QUERY * C * BLOCK * HD * 6, bytes_accessed=1 << 20, transcendentals=HALF * QUERY * C * BLOCK
         ),
         name="ask",
-    )(host, source, lengths, query, rows)
+    )(host, source, meta, query, rows)
 
 
 def merge_kernel(received, out):
@@ -299,51 +300,49 @@
     )(shares)
 
 
-def encode_kernel(host, lengths, query, key, value, anchor, *rest):
+def encode_kernel(host, meta, query, key, value, anchor, *rest):
     out, own_values, anchor_values = rest[-3:]
-
-    @pl.when(pl.program_id(0) == 0)
-    def _():
-        own_values[...] = with_ones(value[...])
-        anchor_values[...] = with_ones(anchor[BLOCK:, :])
-
-    own_len = lengths[host[0]]
-    anchor_len = jnp.where(host[0] > 0, lengths[0], 0)
+    own_values[...] = with_ones(value[...])
+    anchor_values[...] = with_ones(anchor[BLOCK:, :])
+    own_len = meta[host[0] % C]
+    anchor_len = jnp.where(host[0] > 0, meta[C], 0)
     half = BLOCK // 2
-    for tile in range(2):
-        rows = slice(tile * half, (tile + 1) * half)
-        parts = [
-            (key[rows, :], own_values[rows, :], causal(half)),
-            (anchor[:BLOCK, :], anchor_values[...], column_ids(half, BLOCK) < anchor_len),
-        ]
-        if tile:
-            parts.append((key[:half, :], own_values[:half, :], None))
-        _, numer, denom = weigh(query[rows, :], parts)
-        live = lax.broadcasted_iota(jnp.int32, (half, HD), 0) + tile * half < own_len
-        out[rows, :] = jnp.where(live, numer / denom, 0.0).astype(BF16)
-
-
-def encode(host, lengths, query, key, value, anchor, first, count, done=None):
-    whole = pl.BlockSpec((BLOCK, HD), lambda h: (0, 0))
-    heads = pl.BlockSpec((BLOCK, HD), lambda h: (0, h + first))
+    for head in range(out.shape[1] // HD):
+        columns = slice(head * HD, (head + 1) * HD)
+        for tile in range(2):
+            rows = slice(tile * half, (tile + 1) * half)
+            parts = [
+                (key[rows, :], own_values[rows, :], causal(half)),
+                (anchor[:BLOCK, :], anchor_values[...], column_ids(half, BLOCK) < anchor_len),
+            ]
+            if tile:
+                parts.append((key[:half, :], own_values[:half, :], None))
+            _, numer, denom = weigh(query[rows, columns], parts)
+            live = lax.broadcasted_iota(jnp.int32, (half, HD), 0) + tile * half < own_len
+            out[rows, columns] = jnp.where(live, numer / denom, 0.0).astype(BF16)
+
+
+def encode(host, meta, query, key, value, anchor, part, parts, done=None):
+    whole = pl.BlockSpec((BLOCK, HD), lambda i: (0, 0))
+    heads = pl.BlockSpec((BLOCK, HEADS // parts * HD), lambda i: (0, part))
     given = () if done is None else (done,)
     return pl.pallas_call(
         encode_kernel,
         out_shape=jax.ShapeDtypeStruct(query.shape, BF16),
-        grid=(count,),
-        in_specs=[smem(), smem(), heads, whole, whole, pl.BlockSpec((2 * BLOCK, HD), lambda h: (0, 0))]
-        + [pl.BlockSpec(memory_space=pl.ANY)] * len(given),
+        grid=(1,),
+        in_specs=[smem(), smem(), heads, whole, whole, pl.BlockSpec((2 * BLOCK, HD), lambda i: (0, 0))]
+        + [anywhere()] * len(given),
         out_specs=heads,
         scratch_shapes=[pltpu.VMEM((BLOCK, 2 * HD), BF16)] * 2,
         input_output_aliases={6: 0} if given else {},
         compiler_params=params(),
         cost_estimate=pl.CostEstimate(
-            flops=count * BLOCK * BLOCK * HD * 10,
-            bytes_accessed=5 * BLOCK * count * HD,
-            transcendentals=count * BLOCK * BLOCK * 2,
+            flops=HEADS // parts * BLOCK * BLOCK * HD * 10,
+            bytes_accessed=5 * BLOCK * HEADS // parts * HD,
+            transcendentals=HEADS // parts * BLOCK * BLOCK * 2,
         ),
         name="encode",
-    )(host, lengths, query, key, value, anchor, *given)
+    )(host, meta, query, key, value, anchor, *given)
 
 
 def body(
@@ -361,25 +360,38 @@
     core = lax.axis_index("c")
     host = lax.axis_index(("z", "x", "c")).astype(jnp.int32)[None]
 
-    send, keep = pack(host, request_query, context_key, context_value)
-    came = lax.ppermute(send, "c", [(0, 1), (1, 0)])
-    to_chips = choose(host, query_host, keep, came).reshape(pieces, -1, HD)
+    def neither(query, key, value):
+        return blank()
+
+    def request_only(query, key, value):
+        return pack(host, query_host, query, lax.ppermute(query, "c", [(0, 1), (1, 0)]))
+
+    def with_anchor(query, key, value):
+        came = lax.ppermute(query, "c", [(0, 1), (1, 0)])
+        return pack(host, query_host, query, came, key, lax.ppermute(value, "c", [(0, 1)]))
+
+    chip = host[0] // C
+    branch = jnp.where(chip == 0, 2, (chip == query_host[0] // C).astype(jnp.int32))
+    branches = (neither, request_only, with_anchor)
+    to_chips = lax.switch(branch, branches, request_query, context_key, context_value)
+    to_chips = to_chips.reshape(pieces, -1, HD)
     from_chips = lax.all_to_all(to_chips, CHIPS, 0, 0, tiled=True)
     pair_rows = lax.all_gather(join(context_key, context_value, request_key, request_value), "c", axis=0)
     weight_half = lax.dynamic_slice_in_dim(output_weight, (1 - core) * HALF * HD, HALF * HD, 0)
     other_weight = lax.ppermute(weight_half, "c", [(0, 1), (1, 0)])
-    from_chips, pair_rows, other_weight = lax.optimization_barrier((from_chips, pair_rows, other_weight))
+    meta = jnp.concatenate([lax.dynamic_slice_in_dim(block_lengths, host[0] // C * C, C, 0), block_lengths[:1]])
+    from_chips, pair_rows, other_weight, meta = lax.optimization_barrier((from_chips, pair_rows, other_weight, meta))
     part = spread(query_host, from_chips)
     queries = lax.all_to_all(part, CHIPS, 0, 0, tiled=True)
 
-    sums = ask(host, query_host, block_lengths, queries.reshape(Z, X, -1, HD), pair_rows)
+    sums = ask(host, query_host, meta, queries.reshape(Z, X, -1, HD), pair_rows)
     met = lax.all_to_all(sums.reshape(pieces, -1, HD), CHIPS, 0, 0, tiled=True)
     anchor = lax.all_gather(queries[:, piece_rows() :, :].reshape(BLOCK, HD), "c", axis=0, tiled=True)
-    context = (host, block_lengths, context_query, context_key, context_value, anchor)
-    encoded = encode(*context, 0, HEADS // 2)
+    context = (host, meta, context_query, context_key, context_value, anchor)
+    encoded = encode(*context, 0, 2)
     met, encoded = lax.optimization_barrier((met, encoded))
     gathered = lax.all_to_all(merge(met), CHIPS, 0, 0, tiled=True)
-    encoded_context = encode(*context, HEADS // 2, HEADS // 2, encoded)
+    encoded_context = encode(*context, 1, 2, encoded)
     gathered, encoded_context = lax.optimization_barrier((gathered, encoded_context))
     shares = project(host, gathered.reshape(Z, X, -1, HD), output_weight, other_weight)
     blocks = lax.axis_size("head")

time: 114 us -> 105 us (0.921)
  starting transfers between devices: 33.5 us -> 28.9 us
  Pallas kernels: 20.6 us -> 16.7 us
  waiting for transfers between devices: 15.8 us -> 19.5 us
  blocking collectives: 40.1 us -> 36.7 us
    all_to_all x1, starting transfers between devices: 7.65 us -> 4.01 us  [body(): from_chips = lax.all_to_all(to_chips, CHIPS, 0, 0, tiled=True)]
    pallas_call x2, Pallas kernels: 12.4 us -> 9.05 us  [encode(): pl.pallas_call(encode_kernel, out_shape=jax.ShapeDtypeStruct(query.shape,...]
    all_to_all x1, blocking collectives: 16.5 us -> 13.2 us  [body(): lax.all_to_all(shares.reshape(C * blocks, -1, HD), ('c', 'head'), 0, 0, t...]
    all_to_all x1, waiting for transfers between devices: 0.88 us -> 2.59 us  [body(): met = lax.all_to_all(sums.reshape(pieces, -1, HD), CHIPS, 0, 0, tiled=True)]
    all_to_all x1, starting transfers between devices: 8.63 us -> 7.09 us  [body(): gathered = lax.all_to_all(merge(met), CHIPS, 0, 0, tiled=True)]
    ppermute x1 -> x2, starting transfers between devices: 8.77 us -> 10.1 us  [the longest x1 8.79 us: with_anchor(): came = lax.ppermute(query, 'c', [(0, 1), (1, 0)])]
    ppermute x1 -> x2, waiting for transfers between devices: 0.89 us -> 2.16 us  [the longest x1 2.15 us: with_anchor(): lax.ppermute(value, 'c', [(0, 1)])]
    pallas_call x2 -> x1, Pallas kernels: 2.95 us -> 2.54 us  [pack(): pl.pallas_call(pack_kernel, out_shape=jax.ShapeDtypeStruct(shape, BF16),...]
  transfers between devices with their start and end apart: 5 -> 6, of which waited for: 4 -> 4; matrix products, arithmetic and copies ran while one was open for 0% -> 0% of each run, Pallas kernels for 11% -> 9%
where the time goes in v3:
time: 105 us; the launch traced here: 104 us
  blocking collectives  36.7 us (35%)
  starting transfers between devices  28.9 us (28%)
  waiting for transfers between devices  19.5 us (19%)
  Pallas kernels  16.7 us (16%)
  between operations  1.47 us (1%)
    all_to_all x1, blocking collectives, body(): queries = lax.all_to_all(part, CHIPS, 0, 0, tiled=True)  17.5 us
    all_to_all x1, blocking collectives, body(): lax.all_to_all(shares.reshape(C * blocks, -1, HD), ('c', 'head'), 0, 0, t...  13.2 us
    pallas_call x2, Pallas kernels, encode(): pl.pallas_call(encode_kernel, out_shape=jax.ShapeDtypeStruct(query.shape,...  9.05 us
    all_to_all x1, waiting for transfers between devices, body(): from_chips = lax.all_to_all(to_chips, CHIPS, 0, 0, tiled=True)  8.95 us
    ppermute x1, starting transfers between devices, with_anchor(): came = lax.ppermute(query, 'c', [(0, 1), (1, 0)])  8.79 us
    all_to_all x1, starting transfers between devices, body(): gathered = lax.all_to_all(merge(met), CHIPS, 0, 0, tiled=True)  7.09 us
    all_to_all x1, waiting for transfers between devices, body(): gathered = lax.all_to_all(merge(met), CHIPS, 0, 0, tiled=True)  5.83 us
    all_to_all x1, starting transfers between devices, body(): met = lax.all_to_all(sums.reshape(pieces, -1, HD), CHIPS, 0, 0, tiled=True)  5.5 us
  transfers between devices with their start and end apart: 6, of which 4 were waited for; matrix products, arithmetic and copies ran while one was open for 0% of the time, Pallas kernels for 9%

profile of v3, /device:TPU:1, one launch (start us, length us, event | category | flops | bytes accessed | tf_op | source)
XLA Modules:
  0.0 104.2 jit_solution(7914917338988602719)
XLA Ops:
  1.3 14.8 %conditional.1 = (bf16[8,4,48,128]{3,2,1,0:T(8,128)(2,1)}) conditional(s32[]{:T(128)} %clamp.3, () %tuple.20, (bf16[256,1024]{1,0:T(8,128)(2,1)}, s32[1]{0:T(128)}, s32[1]{0:T(128)}) %tuple.21, (bf16[256,1024]{1,0:T(8,128)(2,1)}, bf16[512,128]{1,0:T(8,128)(2,1)}, s32[1]{0:T(128)}, s32[1]{0:T(128)}, bf16[512,128]{1,0:T(8,128)(2,1)}) %tuple.22), branch_computations={%region_0.1_spmd, %region_1.2_spmd, %region_2.3_spmd} | conditional | bytes 2621528 | solution.py:376
  1.4 8.8 %collective-permute-start.1 = (bf16[256,1024]{1,0:T(8,128)(2,1)}, bf16[256,1024]{1,0:T(8,128)(2,1)S(1)}, u32[]{:S(2)}, u32[]{:S(2)}) collective-permute-start(bf16[256,1024]{1,0:T(8,128)(2,1)} %get-tuple-element.25.query), channel_id=1, source_target_pairs={{0,8},{8,0},{1,9},{9,1},{2,10},{10,2},{3,11},{11,3},{4,12},{12,4},... | collective-permute-start | bytes 1572872 | tf_op jit(solution)/shard_map/cond/branch_2_fun/ppermute | solution.py:370
  10.2 1.3 %collective-permute-start.2 = (bf16[512,128]{1,0:T(8,128)(2,1)}, bf16[512,128]{1,0:T(8,128)(2,1)S(1)}, u32[]{:S(2)}, u32[]{:S(2)}) collective-permute-start(bf16[512,128]{1,0:T(8,128)(2,1)} %get-tuple-element.27), channel_id=1, source_target_pairs={{0,8},{1,9},{2,10},{3,11},{4,12},{5,13},{6,14},{7,15},{16,24},{17,... | collective-permute-start | bytes 393224 | tf_op jit(solution)/shard_map/cond/branch_2_fun/ppermute | solution.py:371
  11.5 2.2 %collective-permute-done.2.rest_1_ = bf16[512,128]{1,0:T(8,128)(2,1)S(1)} collective-permute-done((bf16[512,128]{1,0:T(8,128)(2,1)}, bf16[512,128]{1,0:T(8,128)(2,1)S(1)}, u32[]{:S(2)}, u32[]{:S(2)}) %collective-permute-start.2) | collective-permute-done | bytes 131104 | tf_op jit(solution)/shard_map/cond/branch_2_fun/ppermute | solution.py:371
  13.6 0.0 collective-permute-done.1.came
  13.6 2.5 %pack.3 = bf16[8,4,48,128]{3,2,1,0:T(8,128)(2,1)} custom-call(s32[1]{0:T(128)} %get-tuple-element.23.host, s32[1]{0:T(128)} %get-tuple-element.24.source, bf16[256,1024]{1,0:T(8,128)(2,1)} %get-tuple-element.25.query, bf16[256,1024]{1,0:T(8,128)(2,1)S(1)} %collective-permute-done.1.came, bf16[512,128]{1,0:T(8,128)(2,1)} %get-tuple-element.26.rest_0_, ...), custom_call_target="tpu_custom_call" | custom-call | tf_op jit(solution)/shard_map/cond/branch_2_fun/pack/pallas_call | solution.py:102
  16.1 0.0 copy-start
  16.2 0.0 copy-start.5
  16.2 4.0 %all-to-all-start = ((bf16[32,48,128]{2,1,0:T(8,128)(2,1)}), bf16[32,48,128]{2,1,0:T(8,128)(2,1)S(1)}, u32[]{:S(2)}, u32[]{:S(2)}) async-start(bf16[32,48,128]{2,1,0:T(8,128)(2,1)} %bitcast.2), calls=%async_computation | async-start | bytes 786432 | tf_op jit(solution)/shard_map/all_to_all | solution.py:378
  20.2 0.0 copy-done
  20.2 0.0 copy-start.1
  20.2 0.0 copy-start.2
  20.2 0.0 copy-start.4
  20.2 2.2 %collective-permute-start.3 = (bf16[512,128]{1,0:T(8,128)(2,1)S(1)}, bf16[512,128]{1,0:T(8,128)(2,1)S(1)}, u32[]{:S(2)}, u32[]{:S(2)}) collective-permute-start(bf16[512,128]{1,0:T(8,128)(2,1)S(1)} %constant_dynamic-slice_fusion), channel_id=1, source_target_pairs={{0,8},{8,0},{1,9},{9,1},{2,10},{10,2},{3,11},{11,3},{4,12},{12,4},... | collective-permute-start | bytes 393224 | tf_op jit(solution)/shard_map/ppermute | solution.py:381
  22.4 0.0 copy-done.5
  22.4 0.0 copy-done.1
  22.5 0.0 copy-done.2
  22.5 0.0 copy-done.4
  22.5 2.4 %all-gather = bf16[3072,128]{1,0:T(8,128)(2,1)S(1)} all-gather(bf16[1536,128]{1,0:T(8,128)(2,1)S(1)} %join.1), channel_id=2, replica_groups=mesh['z'=8,'x'=4,'c'=2,'head'=8] {'c'}, dimensions={0}, use_global_device_ids=true | all-gather | bytes 1179648 | tf_op jit(solution)/shard_map/all_gather | solution.py:379
  24.9 0.0 copy-start.6
  24.9 0.7 copy-done.6
  25.5 0.1 dynamic_slice.7
  25.6 0.1 pad_add_fusion.meta
  25.7 0.0 collective-permute-done.3.other
  25.7 8.9 %all-to-all-done.asked.anchor = bf16[32,48,128]{2,1,0:T(8,128)(2,1)S(1)} async-done(((bf16[32,48,128]{2,1,0:T(8,128)(2,1)}), bf16[32,48,128]{2,1,0:T(8,128)(2,1)S(1)}, u32[]{:S(2)}, u32[]{:S(2)}) %all-to-all-start) | async-done | bytes 393248 | tf_op jit(solution)/shard_map/all_to_all | solution.py:378
  34.7 0.1 spread.1
  34.7 17.5 %all_to_all.25 = bf16[32,48,128]{2,1,0:T(8,128)(2,1)S(1)} all-to-all(bf16[32,48,128]{2,1,0:T(8,128)(2,1)S(1)} %spread.1), channel_id=1, replica_groups=mesh['z'=8,'x'=4,'c'=2,'head'=8] {'z','x'}, dimensions={0} | all-to-all | bytes 786432 | tf_op jit(solution)/shard_map/all_to_all | solution.py:385
  52.3 3.1 %ask.1 = bf16[8,4,40,128]{3,2,1,0:T(8,128)(2,1)} custom-call(s32[1]{0:T(128)} %bitcast.host, s32[1]{0:T(128)} %copy.16.source, s32[3]{0:T(128)S(1)} %pad_add_fusion.meta, bf16[8,4,48,128]{3,2,1,0:T(8,128)(2,1)S(1)} %bitcast.16, bf16[2,1536,128]{2,1,0:T(8,128)(2,1)S(1)} %bitcast.15), custom_call_target="tpu_custom_call" | custom-call | flops 805306368 | bytes 1048576 | tf_op jit(solution)/shard_map/ask/pallas_call | solution.py:221
  55.4 0.0 copy-start.3
  55.4 5.5 %all-to-all-start.2 = ((bf16[32,40,128]{2,1,0:T(8,128)(2,1)}), bf16[32,40,128]{2,1,0:T(8,128)(2,1)S(1)}, u32[]{:S(2)}, u32[]{:S(2)}) async-start(bf16[32,40,128]{2,1,0:T(8,128)(2,1)} %bitcast.5), calls=%async_computation.2 | async-start | bytes 655360 | tf_op jit(solution)/shard_map/all_to_all | solution.py:388
  60.9 3.6 %all_gather.11.anchor = bf16[1024,128]{1,0:T(8,128)(2,1)S(1)} all-gather(bf16[512,128]{1,0:T(8,128)(2,1)S(1)} %bitcast.18), channel_id=1, replica_groups=mesh['z'=8,'x'=4,'c'=2,'head'=8] {'c'}, dimensions={0}, use_global_device_ids=true | all-gather | bytes 393216 | tf_op jit(solution)/shard_map/all_gather | solution.py:389
  64.5 0.0 copy-done.3
  64.5 4.5 %encode.2.rest_0_ = bf16[512,1024]{1,0:T(8,128)(2,1)} custom-call(s32[1]{0:T(128)} %bitcast.host, s32[3]{0:T(128)S(1)} %pad_add_fusion.meta, bf16[512,1024]{1,0:T(8,128)(2,1)S(1)} %copy-done.3, bf16[512,128]{1,0:T(8,128)(2,1)S(1)} %copy-done.4, bf16[512,128]{1,0:T(8,128)(2,1)S(1)} %copy-done.5, bf16[1024,128]{1,0:T(8,128)(2,1)S(1)} %all_gather.11.anchor), custom_call_target="tpu_custom_call" | custom-call | flops 1342177280 | bytes 1310720 | tf_op jit(solution)/shard_map/encode/pallas_call | solution.py:329
  69.0 2.6 %all-to-all-done.2.received = bf16[32,40,128]{2,1,0:T(8,128)(2,1)S(1)} async-done(((bf16[32,40,128]{2,1,0:T(8,128)(2,1)}), bf16[32,40,128]{2,1,0:T(8,128)(2,1)S(1)}, u32[]{:S(2)}, u32[]{:S(2)}) %all-to-all-start.2) | async-done | bytes 327712 | tf_op jit(solution)/shard_map/all_to_all | solution.py:388
  71.6 1.0 %merge.1 = bf16[32,32,128]{2,1,0:T(8,128)(2,1)} custom-call(bf16[32,40,128]{2,1,0:T(8,128)(2,1)S(1)} %all-to-all-done.2.received), custom_call_target="tpu_custom_call" | custom-call | tf_op jit(solution)/shard_map/merge/pallas_call | solution.py:254
  72.7 7.1 %all-to-all-start.3 = ((bf16[32,32,128]{2,1,0:T(8,128)(2,1)}), bf16[32,32,128]{2,1,0:T(8,128)(2,1)S(1)}, u32[]{:S(2)}, u32[]{:S(2)}) async-start(bf16[32,32,128]{2,1,0:T(8,128)(2,1)} %merge.1), calls=%async_computation.3 | async-start | bytes 524288 | tf_op jit(solution)/shard_map/all_to_all | solution.py:393
  79.8 4.5 %encode.3 = bf16[512,1024]{1,0:T(8,128)(2,1)} custom-call(s32[1]{0:T(128)} %bitcast.host, s32[3]{0:T(128)S(1)} %pad_add_fusion.meta, bf16[512,1024]{1,0:T(8,128)(2,1)S(1)} %copy-done.3, bf16[512,128]{1,0:T(8,128)(2,1)S(1)} %copy-done.4, bf16[512,128]{1,0:T(8,128)(2,1)S(1)} %copy-done.5, ...), custom_call_target="tpu_custom_call", output_to_operand_aliasing={{}: (6, {})} | custom-call | flops 1342177280 | bytes 1310720 | tf_op jit(solution)/shard_map/encode/pallas_call | solution.py:329
  84.3 5.8 %all-to-all-done.3 = bf16[32,32,128]{2,1,0:T(8,128)(2,1)S(1)} async-done(((bf16[32,32,128]{2,1,0:T(8,128)(2,1)}), bf16[32,32,128]{2,1,0:T(8,128)(2,1)S(1)}, u32[]{:S(2)}, u32[]{:S(2)}) %all-to-all-start.3) | async-done | bytes 262176 | tf_op jit(solution)/shard_map/all_to_all | solution.py:393
  90.1 0.3 project.1
  90.4 13.2 %all_to_all.26.shares = bf16[16,32,128]{2,1,0:T(8,128)(2,1)S(1)} all-to-all(bf16[16,32,128]{2,1,0:T(8,128)(2,1)S(1)} %bitcast.17), channel_id=1, replica_groups=mesh['z'=8,'x'=4,'c'=2,'head'=8] {'c','head'}, dimensions={0} | all-to-all | bytes 262144 | tf_op jit(solution)/shard_map/all_to_all | solution.py:398
  103.6 0.6 total.1
  (3 shorter events, 0.1 us)
Async XLA Ops:
  1.4 12.3 %collective-permute-start.1 = (bf16[256,1024]{1,0:T(8,128)(2,1)}, bf16[256,1024]{1,0:T(8,128)(2,1)S(1)}, u32[]{:S(2)}, u32[]{:S(2)}) collective-permute-start(bf16[256,1024]{1,0:T(8,128)(2,1)} %get-tuple-element.25.query), channel_id=1, source_target_pairs={{0,8},{8,0},{1,9},{9,1},{2,10},{10,2},{3,11},{11,3},{4,12},{12,4},... | collective-permute-start | bytes 1572872 | tf_op jit(solution)/shard_map/cond/branch_2_fun/ppermute | solution.py:370
  10.2 3.5 %collective-permute-start.2 = (bf16[512,128]{1,0:T(8,128)(2,1)}, bf16[512,128]{1,0:T(8,128)(2,1)S(1)}, u32[]{:S(2)}, u32[]{:S(2)}) collective-permute-start(bf16[512,128]{1,0:T(8,128)(2,1)} %get-tuple-element.27), channel_id=1, source_target_pairs={{0,8},{1,9},{2,10},{3,11},{4,12},{5,13},{6,14},{7,15},{16,24},{17,... | collective-permute-start | bytes 393224 | tf_op jit(solution)/shard_map/cond/branch_2_fun/ppermute | solution.py:371
  16.1 4.0 %copy-start = (bf16[1024,128]{1,0:T(8,128)(2,1)S(1)}, bf16[1024,128]{1,0:T(8,128)(2,1)}, u32[]{:S(2)}) copy-start(bf16[1024,128]{1,0:T(8,128)(2,1)} %weight.1) | copy-start | bytes 786436
  16.2 6.3 %copy-start.5 = (bf16[512,128]{1,0:T(8,128)(2,1)S(1)}, bf16[512,128]{1,0:T(8,128)(2,1)}, u32[]{:S(2)}) copy-start(bf16[512,128]{1,0:T(8,128)(2,1)} %value.3) | copy-start | bytes 393220
  16.2 18.5 %all-to-all-start = ((bf16[32,48,128]{2,1,0:T(8,128)(2,1)}), bf16[32,48,128]{2,1,0:T(8,128)(2,1)S(1)}, u32[]{:S(2)}, u32[]{:S(2)}) async-start(bf16[32,48,128]{2,1,0:T(8,128)(2,1)} %bitcast.2), calls=%async_computation | async-start | bytes 786432 | tf_op jit(solution)/shard_map/all_to_all | solution.py:378
  20.2 2.3 %copy-start.1 = (bf16[256,128]{1,0:T(8,128)(2,1)S(1)}, bf16[256,128]{1,0:T(8,128)(2,1)}, u32[]{:S(2)}) copy-start(bf16[256,128]{1,0:T(8,128)(2,1)} %refs_2_.1) | copy-start | bytes 196612
  20.2 2.3 %copy-start.2 = (bf16[256,128]{1,0:T(8,128)(2,1)S(1)}, bf16[256,128]{1,0:T(8,128)(2,1)}, u32[]{:S(2)}) copy-start(bf16[256,128]{1,0:T(8,128)(2,1)} %refs_3_.1) | copy-start | bytes 196612
  20.2 2.3 %copy-start.4 = (bf16[512,128]{1,0:T(8,128)(2,1)S(1)}, bf16[512,128]{1,0:T(8,128)(2,1)}, u32[]{:S(2)}) copy-start(bf16[512,128]{1,0:T(8,128)(2,1)} %key.3) | copy-start | bytes 393220
  20.2 5.5 %collective-permute-start.3 = (bf16[512,128]{1,0:T(8,128)(2,1)S(1)}, bf16[512,128]{1,0:T(8,128)(2,1)S(1)}, u32[]{:S(2)}, u32[]{:S(2)}) collective-permute-start(bf16[512,128]{1,0:T(8,128)(2,1)S(1)} %constant_dynamic-slice_fusion), channel_id=1, source_target_pairs={{0,8},{8,0},{1,9},{9,1},{2,10},{10,2},{3,11},{11,3},{4,12},{12,4},... | collective-permute-start | bytes 393224 | tf_op jit(solution)/shard_map/ppermute | solution.py:381
  24.9 0.7 copy-start.6
  55.4 9.1 %copy-start.3 = (bf16[512,1024]{1,0:T(8,128)(2,1)S(1)}, bf16[512,1024]{1,0:T(8,128)(2,1)}, u32[]{:S(2)}) copy-start(bf16[512,1024]{1,0:T(8,128)(2,1)} %query.3) | copy-start | bytes 3145732
  55.4 16.3 %all-to-all-start.2 = ((bf16[32,40,128]{2,1,0:T(8,128)(2,1)}), bf16[32,40,128]{2,1,0:T(8,128)(2,1)S(1)}, u32[]{:S(2)}, u32[]{:S(2)}) async-start(bf16[32,40,128]{2,1,0:T(8,128)(2,1)} %bitcast.5), calls=%async_computation.2 | async-start | bytes 655360 | tf_op jit(solution)/shard_map/all_to_all | solution.py:388
  72.7 17.5 %all-to-all-start.3 = ((bf16[32,32,128]{2,1,0:T(8,128)(2,1)}), bf16[32,32,128]{2,1,0:T(8,128)(2,1)S(1)}, u32[]{:S(2)}, u32[]{:S(2)}) async-start(bf16[32,32,128]{2,1,0:T(8,128)(2,1)} %merge.1), calls=%async_computation.3 | async-start | bytes 524288 | tf_op jit(solution)/shard_map/all_to_all | solution.py:393

commit v4 on v3

--- a/solution.py
+++ b/solution.py
@@ -1,3 +1,5 @@
+import functools
+
 import jax
 import jax.numpy as jnp
 from jax import lax
@@ -71,42 +73,77 @@
     return piece_rows() // GROUPS
 
 
-def pack_kernel(host, source, query, came, *rest):
-    anchors, out = rest[:-1], rest[-1]
+def pack_kernel(with_request, with_anchor, host, source, *refs):
+    refs = list(refs)
     core = host[0] % C
+    query, came = (refs.pop(0), refs.pop(0)) if with_request else (None, None)
+    key, value = (refs.pop(0), refs.pop(0)) if with_anchor else (None, None)
+    out, query_half, packed, load_sems, store_sems = refs
     first = pl.multiple_of(core * HALF * HD, HALF * HD)
-
-    def put(rows):
+    split = piece_rows()
+
+    def put(head, rows, column):
+        packed[:, head, :split, :] = rows[:, pl.ds(column, HD)].reshape(Z, split, HD)
+        store(head, (slice(None), head, slice(0, split))).start()
+
+    def store(index, part):
+        return pltpu.make_async_copy(packed.at[part], out.at[part], store_sems.at[index])
+
+    if with_request:
+        here = source[0] % C == core
+
+        @pl.when(here)
+        def _():
+            loads = [
+                pltpu.make_async_copy(
+                    query.at[:, pl.ds(first + head * HD, HD)],
+                    query_half.at[:, pl.ds(head * HD, HD)],
+                    load_sems.at[head],
+                )
+                for head in range(HALF)
+            ]
+            for load in loads:
+                load.start()
+            for head, load in enumerate(loads):
+                load.wait()
+                put(head, query_half, head * HD)
+
+        @pl.when(jnp.logical_not(here))
+        def _():
+            for head in range(HALF):
+                put(head, came, first + head * HD)
+
+    if with_anchor:
+        for index, rows in enumerate((key, value)):
+
+            @pl.when(core == index)
+            def _():
+                packed[:, :, split:, :] = rows[...].reshape(Z, X, anchor_rows(), HD)
+
+        anchor_part = (slice(None), slice(None), slice(split, packed.shape[2]))
+        store(HALF, anchor_part).start()
+        store(HALF, anchor_part).wait()
+    if with_request:
         for head in range(HALF):
-            out[:, head, : piece_rows(), :] = rows[:, pl.ds(first + head * HD, HD)].reshape(Z, piece_rows(), HD)
-
-    here = source[0] % C == core
-
-    @pl.when(here)
-    def _():
-        put(query)
-
-    @pl.when(jnp.logical_not(here))
-    def _():
-        put(came)
-
-    for index, rows in enumerate(anchors):
-
-        @pl.when(core == index)
-        def _():
-            out[:, :, piece_rows() :, :] = rows[...].reshape(Z, X, anchor_rows(), HD)
-
-
-def pack(host, source, *arrays):
+            store(head, (slice(None), head, slice(0, split))).wait()
+
+
+def pack(host, source, request, anchor):
     shape = (Z, X, piece_rows() + anchor_rows(), HD)
     return pl.pallas_call(
-        pack_kernel,
+        functools.partial(pack_kernel, bool(request), bool(anchor)),
         out_shape=jax.ShapeDtypeStruct(shape, BF16),
-        in_specs=[smem()] * 2 + [vmem()] * len(arrays),
-        out_specs=vmem(),
+        in_specs=[smem()] * 2 + [anywhere(), vmem()] * bool(request) + [vmem()] * len(anchor),
+        out_specs=anywhere(),
+        scratch_shapes=[
+            pltpu.VMEM((QUERY, HALF * HD), BF16),
+            pltpu.VMEM(shape, BF16),
+            pltpu.SemaphoreType.DMA((HALF,)),
+            pltpu.SemaphoreType.DMA((HALF + 1,)),
+        ],
         compiler_params=params(),
         name="pack",
-    )(host, source, *arrays)
+    )(host, source, *request, *anchor)
 
 
 def blank_kernel(out):
@@ -363,16 +400,21 @@
     def neither(query, key, value):
         return blank()
 
+    def ours_and_theirs(query):
+        return query, lax.ppermute(query, "c", [(0, 1), (1, 0)])
+
     def request_only(query, key, value):
-        return pack(host, query_host, query, lax.ppermute(query, "c", [(0, 1), (1, 0)]))
-
-    def with_anchor(query, key, value):
-        came = lax.ppermute(query, "c", [(0, 1), (1, 0)])
-        return pack(host, query_host, query, came, key, lax.ppermute(value, "c", [(0, 1)]))
+        return pack(host, query_host, ours_and_theirs(query), ())
+
+    def anchor_only(query, key, value):
+        return pack(host, query_host, (), (key, lax.ppermute(value, "c", [(0, 1)])))
+
+    def both(query, key, value):
+        return pack(host, query_host, ours_and_theirs(query), (key, lax.ppermute(value, "c", [(0, 1)])))
 
     chip = host[0] // C
-    branch = jnp.where(chip == 0, 2, (chip == query_host[0] // C).astype(jnp.int32))
-    branches = (neither, request_only, with_anchor)
+    branch = (chip == query_host[0] // C).astype(jnp.int32) + 2 * (chip == 0).astype(jnp.int32)
+    branches = (neither, request_only, anchor_only, both)
     to_chips = lax.switch(branch, branches, request_query, context_key, context_value)
     to_chips = to_chips.reshape(pieces, -1, HD)
     from_chips = lax.all_to_all(to_chips, CHIPS, 0, 0, tiled=True)

time: 105 us -> 104 us (level)
  starting transfers between devices: 28.9 us -> 20.1 us
  waiting for transfers between devices: 19.5 us -> 25.3 us
  blocking collectives: 36.7 us -> 39.1 us
    ppermute x2 -> x1, starting transfers between devices: 10.1 us -> 1.29 us  [anchor_only(): return pack(host, query_host, (), (key, lax.ppermute(value, 'c', [(0, 1)])))]
    ppermute x2 -> x1, waiting for transfers between devices: 2.16 us -> 7.91 us  [anchor_only(): return pack(host, query_host, (), (key, lax.ppermute(value, 'c', [(0, 1)])))]
    all_to_all x1, blocking collectives: 13.2 us -> 15.6 us  [body(): lax.all_to_all(shares.reshape(C * blocks, -1, HD), ('c', 'head'), 0, 0, t...]
  transfers between devices with their start and end apart: 6 -> 5, of which waited for: 4 -> 4; matrix products, arithmetic and copies ran while one was open for 0% -> 0% of each run, Pallas kernels for 9% -> 9%
where the time goes in v4:
time: 104 us; the launch traced here: 103 us
  blocking collectives  39.1 us (38%)
  waiting for transfers between devices  25.3 us (24%)
  starting transfers between devices  20.1 us (19%)
  Pallas kernels  16.5 us (16%)
  between operations  1.49 us (1%)
    all_to_all x1, blocking collectives, body(): queries = lax.all_to_all(part, CHIPS, 0, 0, tiled=True)  17.5 us
    all_to_all x1, blocking collectives, body(): lax.all_to_all(shares.reshape(C * blocks, -1, HD), ('c', 'head'), 0, 0, t...  15.6 us
    pallas_call x2, Pallas kernels, encode(): pl.pallas_call(encode_kernel, out_shape=jax.ShapeDtypeStruct(query.shape,...  9.05 us
    all_to_all x1, waiting for transfers between devices, body(): from_chips = lax.all_to_all(to_chips, CHIPS, 0, 0, tiled=True)  8.95 us
    ppermute x1, waiting for transfers between devices, anchor_only(): return pack(host, query_host, (), (key, lax.ppermute(value, 'c', [(0, 1)])))  7.91 us
    all_to_all x1, starting transfers between devices, body(): gathered = lax.all_to_all(merge(met), CHIPS, 0, 0, tiled=True)  7.09 us
    all_to_all x1, waiting for transfers between devices, body(): gathered = lax.all_to_all(merge(met), CHIPS, 0, 0, tiled=True)  5.83 us
    all_to_all x1, starting transfers between devices, body(): met = lax.all_to_all(sums.reshape(pieces, -1, HD), CHIPS, 0, 0, tiled=True)  5.5 us
  transfers between devices with their start and end apart: 5, of which 4 were waited for; matrix products, arithmetic and copies ran while one was open for 0% of the time, Pallas kernels for 9%

profile of v4, /device:TPU:1, one launch (start us, length us, event | category | flops | bytes accessed | tf_op | source)
XLA Modules:
  0.0 103.4 jit_solution(5544423911563021680)
XLA Ops:
  1.3 11.5 %conditional.1 = (bf16[8,4,48,128]{3,2,1,0:T(8,128)(2,1)}) conditional(s32[]{:T(128)} %clamp.3, () %tuple.23, (bf16[256,1024]{1,0:T(8,128)(2,1)}, s32[1]{0:T(128)}, s32[1]{0:T(128)}) %tuple.24, (bf16[512,128]{1,0:T(8,128)(2,1)}, s32[1]{0:T(128)}, s32[1]{0:T(128)}, bf16[512,128]{1,0:T(8,128)(2,1)}) %tuple.25, ...), branch_computations={%region_0.1_spmd, %region_1.2_spmd, %region_2.3_spmd, %region_3.4_... | conditional | bytes 2621528 | solution.py:418
  1.3 1.3 %collective-permute-start.1 = (bf16[512,128]{1,0:T(8,128)(2,1)}, bf16[512,128]{1,0:T(8,128)(2,1)S(1)}, u32[]{:S(2)}, u32[]{:S(2)}) collective-permute-start(bf16[512,128]{1,0:T(8,128)(2,1)} %get-tuple-element.35), channel_id=1, source_target_pairs={{0,8},{1,9},{2,10},{3,11},{4,12},{5,13},{6,14},{7,15},{16,24},{17,... | collective-permute-start | bytes 393224 | tf_op jit(solution)/shard_map/cond/branch_2_fun/ppermute | solution.py:410
  2.6 7.9 %collective-permute-done.1.refs_1_ = bf16[512,128]{1,0:T(8,128)(2,1)S(1)} collective-permute-done((bf16[512,128]{1,0:T(8,128)(2,1)}, bf16[512,128]{1,0:T(8,128)(2,1)S(1)}, u32[]{:S(2)}, u32[]{:S(2)}) %collective-permute-start.1) | collective-permute-done | bytes 131104 | tf_op jit(solution)/shard_map/cond/branch_2_fun/ppermute | solution.py:410
  10.6 2.3 %pack.4 = bf16[8,4,48,128]{3,2,1,0:T(8,128)(2,1)} custom-call(s32[1]{0:T(128)} %get-tuple-element.32.host, s32[1]{0:T(128)} %get-tuple-element.33.source, bf16[512,128]{1,0:T(8,128)(2,1)} %get-tuple-element.34.refs_0_, bf16[512,128]{1,0:T(8,128)(2,1)S(1)} %collective-permute-done.1.refs_1_), custom_call_target="tpu_custom_call" | custom-call | tf_op jit(solution)/shard_map/cond/branch_2_fun/pack/pallas_call | solution.py:133
  12.9 0.0 copy-start
  12.9 0.0 copy-start.5
  12.9 4.0 %all-to-all-start = ((bf16[32,48,128]{2,1,0:T(8,128)(2,1)}), bf16[32,48,128]{2,1,0:T(8,128)(2,1)S(1)}, u32[]{:S(2)}, u32[]{:S(2)}) async-start(bf16[32,48,128]{2,1,0:T(8,128)(2,1)} %bitcast.2), calls=%async_computation | async-start | bytes 786432 | tf_op jit(solution)/shard_map/all_to_all | solution.py:420
  16.9 0.0 copy-done
  16.9 0.0 copy-start.1
  16.9 0.0 copy-start.2
  17.0 0.0 copy-start.4
  17.0 2.2 %collective-permute-start.4 = (bf16[512,128]{1,0:T(8,128)(2,1)S(1)}, bf16[512,128]{1,0:T(8,128)(2,1)S(1)}, u32[]{:S(2)}, u32[]{:S(2)}) collective-permute-start(bf16[512,128]{1,0:T(8,128)(2,1)S(1)} %constant_dynamic-slice_fusion), channel_id=1, source_target_pairs={{0,8},{8,0},{1,9},{9,1},{2,10},{10,2},{3,11},{11,3},{4,12},{12,4},... | collective-permute-start | bytes 393224 | tf_op jit(solution)/shard_map/ppermute | solution.py:423
  19.2 0.0 copy-done.5
  19.2 0.0 copy-done.1
  19.2 0.0 copy-done.2
  19.2 0.0 copy-done.4
  19.3 2.4 %all-gather = bf16[3072,128]{1,0:T(8,128)(2,1)S(1)} all-gather(bf16[1536,128]{1,0:T(8,128)(2,1)S(1)} %join.1), channel_id=2, replica_groups=mesh['z'=8,'x'=4,'c'=2,'head'=8] {'c'}, dimensions={0}, use_global_device_ids=true | all-gather | bytes 1179648 | tf_op jit(solution)/shard_map/all_gather | solution.py:421
  21.6 0.0 copy-start.6
  21.6 0.7 copy-done.6
  22.3 0.1 dynamic_slice.7
  22.4 0.1 pad_add_fusion.meta
  22.5 0.0 collective-permute-done.4.other
  22.5 9.0 %all-to-all-done.asked.anchor = bf16[32,48,128]{2,1,0:T(8,128)(2,1)S(1)} async-done(((bf16[32,48,128]{2,1,0:T(8,128)(2,1)}), bf16[32,48,128]{2,1,0:T(8,128)(2,1)S(1)}, u32[]{:S(2)}, u32[]{:S(2)}) %all-to-all-start) | async-done | bytes 393248 | tf_op jit(solution)/shard_map/all_to_all | solution.py:420
  31.4 0.1 spread.1
  31.5 17.5 %all_to_all.25 = bf16[32,48,128]{2,1,0:T(8,128)(2,1)S(1)} all-to-all(bf16[32,48,128]{2,1,0:T(8,128)(2,1)S(1)} %spread.1), channel_id=1, replica_groups=mesh['z'=8,'x'=4,'c'=2,'head'=8] {'z','x'}, dimensions={0} | all-to-all | bytes 786432 | tf_op jit(solution)/shard_map/all_to_all | solution.py:427
  49.0 3.1 %ask.1 = bf16[8,4,40,128]{3,2,1,0:T(8,128)(2,1)} custom-call(s32[1]{0:T(128)} %bitcast.host, s32[1]{0:T(128)} %copy.17.source, s32[3]{0:T(128)S(1)} %pad_add_fusion.meta, bf16[8,4,48,128]{3,2,1,0:T(8,128)(2,1)S(1)} %bitcast.16, bf16[2,1536,128]{2,1,0:T(8,128)(2,1)S(1)} %bitcast.15), custom_call_target="tpu_custom_call" | custom-call | flops 805306368 | bytes 1048576 | tf_op jit(solution)/shard_map/ask/pallas_call | solution.py:258
  52.1 0.0 copy-start.3
  52.1 5.5 %all-to-all-start.2 = ((bf16[32,40,128]{2,1,0:T(8,128)(2,1)}), bf16[32,40,128]{2,1,0:T(8,128)(2,1)S(1)}, u32[]{:S(2)}, u32[]{:S(2)}) async-start(bf16[32,40,128]{2,1,0:T(8,128)(2,1)} %bitcast.5), calls=%async_computation.2 | async-start | bytes 655360 | tf_op jit(solution)/shard_map/all_to_all | solution.py:430
  57.6 3.6 %all_gather.11.anchor = bf16[1024,128]{1,0:T(8,128)(2,1)S(1)} all-gather(bf16[512,128]{1,0:T(8,128)(2,1)S(1)} %bitcast.18), channel_id=1, replica_groups=mesh['z'=8,'x'=4,'c'=2,'head'=8] {'c'}, dimensions={0}, use_global_device_ids=true | all-gather | bytes 393216 | tf_op jit(solution)/shard_map/all_gather | solution.py:431
  61.3 0.0 copy-done.3
  61.3 4.5 %encode.2.rest_0_ = bf16[512,1024]{1,0:T(8,128)(2,1)} custom-call(s32[1]{0:T(128)} %bitcast.host, s32[3]{0:T(128)S(1)} %pad_add_fusion.meta, bf16[512,1024]{1,0:T(8,128)(2,1)S(1)} %copy-done.3, bf16[512,128]{1,0:T(8,128)(2,1)S(1)} %copy-done.4, bf16[512,128]{1,0:T(8,128)(2,1)S(1)} %copy-done.5, bf16[1024,128]{1,0:T(8,128)(2,1)S(1)} %all_gather.11.anchor), custom_call_target="tpu_custom_call" | custom-call | flops 1342177280 | bytes 1310720 | tf_op jit(solution)/shard_map/encode/pallas_call | solution.py:366
  65.8 2.6 %all-to-all-done.2.received = bf16[32,40,128]{2,1,0:T(8,128)(2,1)S(1)} async-done(((bf16[32,40,128]{2,1,0:T(8,128)(2,1)}), bf16[32,40,128]{2,1,0:T(8,128)(2,1)S(1)}, u32[]{:S(2)}, u32[]{:S(2)}) %all-to-all-start.2) | async-done | bytes 327712 | tf_op jit(solution)/shard_map/all_to_all | solution.py:430
  68.4 1.1 %merge.1 = bf16[32,32,128]{2,1,0:T(8,128)(2,1)} custom-call(bf16[32,40,128]{2,1,0:T(8,128)(2,1)S(1)} %all-to-all-done.2.received), custom_call_target="tpu_custom_call" | custom-call | tf_op jit(solution)/shard_map/merge/pallas_call | solution.py:291
  69.4 7.1 %all-to-all-start.3 = ((bf16[32,32,128]{2,1,0:T(8,128)(2,1)}), bf16[32,32,128]{2,1,0:T(8,128)(2,1)S(1)}, u32[]{:S(2)}, u32[]{:S(2)}) async-start(bf16[32,32,128]{2,1,0:T(8,128)(2,1)} %merge.1), calls=%async_computation.3 | async-start | bytes 524288 | tf_op jit(solution)/shard_map/all_to_all | solution.py:435
  76.5 4.5 %encode.3 = bf16[512,1024]{1,0:T(8,128)(2,1)} custom-call(s32[1]{0:T(128)} %bitcast.host, s32[3]{0:T(128)S(1)} %pad_add_fusion.meta, bf16[512,1024]{1,0:T(8,128)(2,1)S(1)} %copy-done.3, bf16[512,128]{1,0:T(8,128)(2,1)S(1)} %copy-done.4, bf16[512,128]{1,0:T(8,128)(2,1)S(1)} %copy-done.5, ...), custom_call_target="tpu_custom_call", output_to_operand_aliasing={{}: (6, {})} | custom-call | flops 1342177280 | bytes 1310720 | tf_op jit(solution)/shard_map/encode/pallas_call | solution.py:366
  81.1 5.8 %all-to-all-done.3 = bf16[32,32,128]{2,1,0:T(8,128)(2,1)S(1)} async-done(((bf16[32,32,128]{2,1,0:T(8,128)(2,1)}), bf16[32,32,128]{2,1,0:T(8,128)(2,1)S(1)}, u32[]{:S(2)}, u32[]{:S(2)}) %all-to-all-start.3) | async-done | bytes 262176 | tf_op jit(solution)/shard_map/all_to_all | solution.py:435
  86.9 0.3 project.1
  87.2 15.6 %all_to_all.26.shares = bf16[16,32,128]{2,1,0:T(8,128)(2,1)S(1)} all-to-all(bf16[16,32,128]{2,1,0:T(8,128)(2,1)S(1)} %bitcast.17), channel_id=1, replica_groups=mesh['z'=8,'x'=4,'c'=2,'head'=8] {'c','head'}, dimensions={0} | all-to-all | bytes 262144 | tf_op jit(solution)/shard_map/all_to_all | solution.py:440
  102.8 0.6 total.1
  (3 shorter events, 0.1 us)
Async XLA Ops:
  1.3 9.2 %collective-permute-start.1 = (bf16[512,128]{1,0:T(8,128)(2,1)}, bf16[512,128]{1,0:T(8,128)(2,1)S(1)}, u32[]{:S(2)}, u32[]{:S(2)}) collective-permute-start(bf16[512,128]{1,0:T(8,128)(2,1)} %get-tuple-element.35), channel_id=1, source_target_pairs={{0,8},{1,9},{2,10},{3,11},{4,12},{5,13},{6,14},{7,15},{16,24},{17,... | collective-permute-start | bytes 393224 | tf_op jit(solution)/shard_map/cond/branch_2_fun/ppermute | solution.py:410
  12.9 4.1 %copy-start = (bf16[1024,128]{1,0:T(8,128)(2,1)S(1)}, bf16[1024,128]{1,0:T(8,128)(2,1)}, u32[]{:S(2)}) copy-start(bf16[1024,128]{1,0:T(8,128)(2,1)} %weight.1) | copy-start | bytes 786436
  12.9 6.3 %copy-start.5 = (bf16[512,128]{1,0:T(8,128)(2,1)S(1)}, bf16[512,128]{1,0:T(8,128)(2,1)}, u32[]{:S(2)}) copy-start(bf16[512,128]{1,0:T(8,128)(2,1)} %value.3) | copy-start | bytes 393220
  12.9 18.5 %all-to-all-start = ((bf16[32,48,128]{2,1,0:T(8,128)(2,1)}), bf16[32,48,128]{2,1,0:T(8,128)(2,1)S(1)}, u32[]{:S(2)}, u32[]{:S(2)}) async-start(bf16[32,48,128]{2,1,0:T(8,128)(2,1)} %bitcast.2), calls=%async_computation | async-start | bytes 786432 | tf_op jit(solution)/shard_map/all_to_all | solution.py:420
  16.9 2.3 %copy-start.1 = (bf16[256,128]{1,0:T(8,128)(2,1)S(1)}, bf16[256,128]{1,0:T(8,128)(2,1)}, u32[]{:S(2)}) copy-start(bf16[256,128]{1,0:T(8,128)(2,1)} %refs_2_.1) | copy-start | bytes 196612
  16.9 2.3 %copy-start.2 = (bf16[256,128]{1,0:T(8,128)(2,1)S(1)}, bf16[256,128]{1,0:T(8,128)(2,1)}, u32[]{:S(2)}) copy-start(bf16[256,128]{1,0:T(8,128)(2,1)} %refs_3_.1) | copy-start | bytes 196612
  17.0 2.3 %copy-start.4 = (bf16[512,128]{1,0:T(8,128)(2,1)S(1)}, bf16[512,128]{1,0:T(8,128)(2,1)}, u32[]{:S(2)}) copy-start(bf16[512,128]{1,0:T(8,128)(2,1)} %key.3) | copy-start | bytes 393220
  17.0 5.5 %collective-permute-start.4 = (bf16[512,128]{1,0:T(8,128)(2,1)S(1)}, bf16[512,128]{1,0:T(8,128)(2,1)S(1)}, u32[]{:S(2)}, u32[]{:S(2)}) collective-permute-start(bf16[512,128]{1,0:T(8,128)(2,1)S(1)} %constant_dynamic-slice_fusion), channel_id=1, source_target_pairs={{0,8},{8,0},{1,9},{9,1},{2,10},{10,2},{3,11},{11,3},{4,12},{12,4},... | collective-permute-start | bytes 393224 | tf_op jit(solution)/shard_map/ppermute | solution.py:423
  21.6 0.7 copy-start.6
  52.1 9.2 %copy-start.3 = (bf16[512,1024]{1,0:T(8,128)(2,1)S(1)}, bf16[512,1024]{1,0:T(8,128)(2,1)}, u32[]{:S(2)}) copy-start(bf16[512,1024]{1,0:T(8,128)(2,1)} %query.3) | copy-start | bytes 3145732
  52.1 16.3 %all-to-all-start.2 = ((bf16[32,40,128]{2,1,0:T(8,128)(2,1)}), bf16[32,40,128]{2,1,0:T(8,128)(2,1)S(1)}, u32[]{:S(2)}, u32[]{:S(2)}) async-start(bf16[32,40,128]{2,1,0:T(8,128)(2,1)} %bitcast.5), calls=%async_computation.2 | async-start | bytes 655360 | tf_op jit(solution)/shard_map/all_to_all | solution.py:430
  69.4 17.5 %all-to-all-start.3 = ((bf16[32,32,128]{2,1,0:T(8,128)(2,1)}), bf16[32,32,128]{2,1,0:T(8,128)(2,1)S(1)}, u32[]{:S(2)}, u32[]{:S(2)}) async-start(bf16[32,32,128]{2,1,0:T(8,128)(2,1)} %merge.1), calls=%async_computation.3 | async-start | bytes 524288 | tf_op jit(solution)/shard_map/all_to_all | solution.py:435

commit v5 on v3

--- a/solution.py
+++ b/solution.py
@@ -1,3 +1,5 @@
+import functools
+
 import jax
 import jax.numpy as jnp
 from jax import lax
@@ -71,42 +73,104 @@
     return piece_rows() // GROUPS
 
 
-def pack_kernel(host, source, query, came, *rest):
-    anchors, out = rest[:-1], rest[-1]
-    core = host[0] % C
+def pack_own_kernel(source_core, query, out, query_half, packed, load_sems, store_sems):
+    core = lax.axis_index("c")
     first = pl.multiple_of(core * HALF * HD, HALF * HD)
 
-    def put(rows):
-        for head in range(HALF):
-            out[:, head, : piece_rows(), :] = rows[:, pl.ds(first + head * HD, HD)].reshape(Z, piece_rows(), HD)
-
-    here = source[0] % C == core
-
-    @pl.when(here)
+    @pl.when(core == source_core)
     def _():
-        put(query)
-
-    @pl.when(jnp.logical_not(here))
+        loads = [
+            pltpu.make_async_copy(
+                query.at[:, pl.ds(first + head * HD, HD)],
+                query_half.at[:, pl.ds(head * HD, HD)],
+                load_sems.at[head],
+            )
+            for head in range(HALF)
+        ]
+        stores = [
+            pltpu.make_async_copy(packed.at[:, head], out.at[:, head, : piece_rows()], store_sems.at[head])
+            for head in range(HALF)
+        ]
+        for load in loads:
+            load.start()
+        for head, (load, store) in enumerate(zip(loads, stores)):
+            load.wait()
+            packed[:, head] = query_half[:, head * HD : (head + 1) * HD].reshape(Z, piece_rows(), HD)
+            store.start()
+        for store in stores:
+            store.wait()
+
+
+def pack_own(source_core, query):
+    return pl.pallas_call(
+        functools.partial(pack_own_kernel, source_core),
+        out_shape=jax.ShapeDtypeStruct((Z, X, piece_rows() + anchor_rows(), HD), BF16),
+        in_specs=[anywhere()],
+        out_specs=anywhere(),
+        scratch_shapes=[
+            pltpu.VMEM((QUERY, HALF * HD), BF16),
+            pltpu.VMEM((Z, HALF, piece_rows(), HD), BF16),
+            pltpu.SemaphoreType.DMA((HALF,)),
+            pltpu.SemaphoreType.DMA((HALF,)),
+        ],
+        compiler_params=params(),
+        name="pack_own",
+    )(query)
+
+
+def pack_came_kernel(source_core, came, given, out, packed, sems):
+    core = lax.axis_index("c")
+    first = pl.multiple_of(core * HALF * HD, HALF * HD)
+
+    @pl.when(core != source_core)
     def _():
-        put(came)
-
-    for index, rows in enumerate(anchors):
-
-        @pl.when(core == index)
+        stores = [
+            pltpu.make_async_copy(packed.at[:, head], out.at[:, head, : piece_rows()], sems.at[head])
+            for head in range(HALF)
+        ]
+        for head, store in enumerate(stores):
+            packed[:, head] = came[:, pl.ds(first + head * HD, HD)].reshape(Z, piece_rows(), HD)
+            store.start()
+        for store in stores:
+            store.wait()
+
+
+def pack_came(source_core, came, packed):
+    return pl.pallas_call(
+        functools.partial(pack_came_kernel, source_core),
+        out_shape=jax.ShapeDtypeStruct(packed.shape, BF16),
+        in_specs=[vmem(), anywhere()],
+        out_specs=anywhere(),
+        input_output_aliases={1: 0},
+        scratch_shapes=[pltpu.VMEM((Z, HALF, piece_rows(), HD), BF16), pltpu.SemaphoreType.DMA((HALF,))],
+        compiler_params=params(),
+        name="pack_came",
+    )(came, packed)
+
+
+def pack_anchor_kernel(key, value, given, out, packed, sem):
+    for index, rows in enumerate((key, value)):
+
+        @pl.when(lax.axis_index("c") == index)
         def _():
-            out[:, :, piece_rows() :, :] = rows[...].reshape(Z, X, anchor_rows(), HD)
-
-
-def pack(host, source, *arrays):
-    shape = (Z, X, piece_rows() + anchor_rows(), HD)
-    return pl.pallas_call(
-        pack_kernel,
-        out_shape=jax.ShapeDtypeStruct(shape, BF16),
-        in_specs=[smem()] * 2 + [vmem()] * len(arrays),
-        out_specs=vmem(),
-        compiler_params=params(),
-        name="pack",
-    )(host, source, *arrays)
+            packed[...] = rows[...].reshape(Z, X, anchor_rows(), HD)
+
+    store = pltpu.make_async_copy(packed, out.at[:, :, piece_rows() :], sem)
+    store.start()
+    store.wait()
+
+
+def pack_anchor(key, value, packed):
+    return pl.pallas_call(
+        pack_anchor_kernel,
+        out_shape=jax.ShapeDtypeStruct(packed.shape, BF16),
+        in_specs=[vmem()] * 2 + [anywhere()],
+        out_specs=anywhere(),
+        input_output_aliases={2: 0},
+        scratch_shapes=[pltpu.VMEM((Z, X, anchor_rows(), HD), BF16), pltpu.SemaphoreType.DMA],
+        compiler_params=params(),
+        name="pack_anchor",
+    )(key, value, packed)
 
 
 def blank_kernel(out):
@@ -178,9 +242,8 @@
     return side
 
 
-def ask_kernel(host, source, meta, query, rows, out, values):
+def ask_kernel(meta, query, rows, out, values):
     split = piece_rows()
-    chip = host[0] // C
     for core in range(C):
         values[core] = with_ones(rows[core, BLOCK : 2 * BLOCK, :])
 
@@ -192,7 +255,7 @@
                 for core in range(C)
             ]
             if own:
-                core = source[0] % C
+                core = meta[C + 2]
                 ask_key = rows[core, 2 * BLOCK : 2 * BLOCK + QUERY, :]
                 ask_value = rows[core, 2 * BLOCK + QUERY :, :]
                 parts.append((ask_key, with_ones(ask_value), causal(QUERY)))
@@ -206,7 +269,7 @@
             coded = jnp.where(lane == 0, high, jnp.where(lane == 1, middle, rest - middle))
             out[:, head, split:, :] = coded.astype(BF16)
 
-    here = source[0] // C == chip
+    here = meta[C + 1] != 0
 
     @pl.when(jnp.logical_not(here))
     def _():
@@ -217,11 +280,11 @@
         run(True)
 
 
-def ask(host, source, meta, query, rows):
+def ask(meta, query, rows):
     return pl.pallas_call(
         ask_kernel,
         out_shape=jax.ShapeDtypeStruct((Z, X, piece_rows() + level_rows(), HD), BF16),
-        in_specs=[smem()] * 3 + [vmem()] * 2,
+        in_specs=[smem()] + [vmem()] * 2,
         out_specs=vmem(),
         scratch_shapes=[pltpu.VMEM((C, BLOCK, 2 * HD), BF16)],
         compiler_params=params(),
@@ -229,7 +292,7 @@
             flops=HALF * QUERY * C * BLOCK * HD * 6, bytes_accessed=1 << 20, transcendentals=HALF * QUERY * C * BLOCK
         ),
         name="ask",
-    )(host, source, meta, query, rows)
+    )(meta, query, rows)
 
 
 def merge_kernel(received, out):
@@ -261,8 +324,8 @@
     )(received)
 
 
-def project_kernel(host, attended, weight, other, out):
-    core = host[0] % C
+def project_kernel(attended, weight, other, out):
+    core = lax.axis_index("c")
     rows = [
         jnp.concatenate([attended[z, x] for x in range(X)], axis=1) for z in range(Z)
     ]
@@ -274,15 +337,15 @@
     out[pl.ds(1 - core, 1)] = others.astype(BF16)[None]
 
 
-def project(host, attended, weight, other):
+def project(attended, weight, other):
     return pl.pallas_call(
         project_kernel,
         out_shape=jax.ShapeDtypeStruct((C, QUERY, HD), BF16),
-        in_specs=[smem()] + [vmem()] * 3,
+        in_specs=[vmem()] * 3,
         out_specs=vmem(),
         compiler_params=params(),
         name="project",
-    )(host, attended, weight, other)
+    )(attended, weight, other)
 
 
 def total_kernel(shares, out):
@@ -300,12 +363,11 @@
     )(shares)
 
 
-def encode_kernel(host, meta, query, key, value, anchor, *rest):
+def encode_kernel(meta, query, key, value, anchor, *rest):
     out, own_values, anchor_values = rest[-3:]
     own_values[...] = with_ones(value[...])
     anchor_values[...] = with_ones(anchor[BLOCK:, :])
-    own_len = meta[host[0] % C]
-    anchor_len = jnp.where(host[0] > 0, meta[C], 0)
+    own_len, anchor_len = meta[lax.axis_index("c")], meta[C]
     half = BLOCK // 2
     for head in range(out.shape[1] // HD):
         columns = slice(head * HD, (head + 1) * HD)
@@ -322,7 +384,7 @@
             out[rows, columns] = jnp.where(live, numer / denom, 0.0).astype(BF16)
 
 
-def encode(host, meta, query, key, value, anchor, part, parts, done=None):
+def encode(meta, query, key, value, anchor, part, parts, done=None):
     whole = pl.BlockSpec((BLOCK, HD), lambda i: (0, 0))
     heads = pl.BlockSpec((BLOCK, HEADS // parts * HD), lambda i: (0, part))
     given = () if done is None else (done,)
@@ -330,11 +392,11 @@
         encode_kernel,
         out_shape=jax.ShapeDtypeStruct(query.shape, BF16),
         grid=(1,),
-        in_specs=[smem(), smem(), heads, whole, whole, pl.BlockSpec((2 * BLOCK, HD), lambda i: (0, 0))]
+        in_specs=[smem(), heads, whole, whole, pl.BlockSpec((2 * BLOCK, HD), lambda i: (0, 0))]
         + [anywhere()] * len(given),
         out_specs=heads,
         scratch_shapes=[pltpu.VMEM((BLOCK, 2 * HD), BF16)] * 2,
-        input_output_aliases={6: 0} if given else {},
+        input_output_aliases={5: 0} if given else {},
         compiler_params=params(),
         cost_estimate=pl.CostEstimate(
             flops=HEADS // parts * BLOCK * BLOCK * HD * 10,
@@ -342,7 +404,7 @@
             transcendentals=HEADS // parts * BLOCK * BLOCK * 2,
         ),
         name="encode",
-    )(host, meta, query, key, value, anchor, *given)
+    )(meta, query, key, value, anchor, *given)
 
 
 def body(
@@ -363,37 +425,51 @@
     def neither(query, key, value):
         return blank()
 
-    def request_only(query, key, value):
-        return pack(host, query_host, query, lax.ppermute(query, "c", [(0, 1), (1, 0)]))
-
-    def with_anchor(query, key, value):
-        came = lax.ppermute(query, "c", [(0, 1), (1, 0)])
-        return pack(host, query_host, query, came, key, lax.ppermute(value, "c", [(0, 1)]))
+    def request_only(source_core, query, key, value):
+        came = lax.ppermute(query, "c", [(source_core, 1 - source_core)])
+        return pack_came(source_core, came, pack_own(source_core, query))
+
+    def with_anchor(packed, key, value):
+        return pack_anchor(key, lax.ppermute(value, "c", [(0, 1)]), packed)
+
+    def anchor_only(query, key, value):
+        return with_anchor(blank(), key, value)
+
+    def both(source_core, query, key, value):
+        return with_anchor(request_only(source_core, query, key, value), key, value)
 
     chip = host[0] // C
-    branch = jnp.where(chip == 0, 2, (chip == query_host[0] // C).astype(jnp.int32))
-    branches = (neither, request_only, with_anchor)
+    here = chip == query_host[0] // C
+    branch = jnp.where(here, 1 + query_host[0] % C, 0) + (C + 1) * (chip == 0).astype(jnp.int32)
+    branches = (
+        (neither,)
+        + tuple(functools.partial(request_only, source_core) for source_core in range(C))
+        + (anchor_only,)
+        + tuple(functools.partial(both, source_core) for source_core in range(C))
+    )
     to_chips = lax.switch(branch, branches, request_query, context_key, context_value)
     to_chips = to_chips.reshape(pieces, -1, HD)
     from_chips = lax.all_to_all(to_chips, CHIPS, 0, 0, tiled=True)
     pair_rows = lax.all_gather(join(context_key, context_value, request_key, request_value), "c", axis=0)
     weight_half = lax.dynamic_slice_in_dim(output_weight, (1 - core) * HALF * HD, HALF * HD, 0)
     other_weight = lax.ppermute(weight_half, "c", [(0, 1), (1, 0)])
-    meta = jnp.concatenate([lax.dynamic_slice_in_dim(block_lengths, host[0] // C * C, C, 0), block_lengths[:1]])
+    anchor_len = jnp.where(host > 0, block_lengths[:1], 0)
+    pair_lens = lax.dynamic_slice_in_dim(block_lengths, chip * C, C, 0)
+    meta = jnp.concatenate([pair_lens, anchor_len, here[None].astype(jnp.int32), query_host % C])
     from_chips, pair_rows, other_weight, meta = lax.optimization_barrier((from_chips, pair_rows, other_weight, meta))
     part = spread(query_host, from_chips)
     queries = lax.all_to_all(part, CHIPS, 0, 0, tiled=True)
 
-    sums = ask(host, query_host, meta, queries.reshape(Z, X, -1, HD), pair_rows)
+    sums = ask(meta, queries.reshape(Z, X, -1, HD), pair_rows)
     met = lax.all_to_all(sums.reshape(pieces, -1, HD), CHIPS, 0, 0, tiled=True)
     anchor = lax.all_gather(queries[:, piece_rows() :, :].reshape(BLOCK, HD), "c", axis=0, tiled=True)
-    context = (host, meta, context_query, context_key, context_value, anchor)
+    context = (meta, context_query, context_key, context_value, anchor)
     encoded = encode(*context, 0, 2)
     met, encoded = lax.optimization_barrier((met, encoded))
     gathered = lax.all_to_all(merge(met), CHIPS, 0, 0, tiled=True)
     encoded_context = encode(*context, 1, 2, encoded)
     gathered, encoded_context = lax.optimization_barrier((gathered, encoded_context))
-    shares = project(host, gathered.reshape(Z, X, -1, HD), output_weight, other_weight)
+    shares = project(gathered.reshape(Z, X, -1, HD), output_weight, other_weight)
     blocks = lax.axis_size("head")
     shares = lax.all_to_all(shares.reshape(C * blocks, -1, HD), ("c", "head"), 0, 0, tiled=True)
     return (encoded_context, total(shares))

time: 105 us -> 109 us (1.038)
  waiting for transfers between devices: 19.5 us -> 26.4 us
  starting transfers between devices: 28.9 us -> 24 us
  blocking collectives: 36.7 us -> 41 us
  Pallas kernels: 16.7 us -> 14.9 us
    ppermute x2 -> x1, starting transfers between devices: 10.1 us -> 1.42 us  [with_anchor(): return pack_anchor(key, lax.ppermute(value, 'c', [(0, 1)]), packed)]
    ppermute x2 -> x1, waiting for transfers between devices: 2.16 us -> 7.9 us  [with_anchor(): return pack_anchor(key, lax.ppermute(value, 'c', [(0, 1)]), packed)]
    all_to_all x1, blocking collectives: 13.2 us -> 17.8 us  [body(): lax.all_to_all(shares.reshape(C * blocks, -1, HD), ('c', 'head'), 0, 0, t...]
    all_to_all x1, starting transfers between devices: 4.01 us -> 8.6 us  [body(): from_chips = lax.all_to_all(to_chips, CHIPS, 0, 0, tiled=True)]
    pallas_call x1 -> x2, Pallas kernels: 2.54 us -> 0.67 us  [the longest x1 0.67 us: pack_anchor(): pl.pallas_call(pack_anchor_kernel, out_shape=jax.ShapeDtypeStruct(packed....]
  transfers between devices with their start and end apart: 6 -> 5, of which waited for: 4 -> 4; matrix products, arithmetic and copies ran while one was open for 0% -> 0% of each run, Pallas kernels for 9% -> 8%
where the time goes in v5:
time: 109 us
  blocking collectives  41 us (38%)
  waiting for transfers between devices  26.4 us (24%)
  starting transfers between devices  24 us (22%)
  Pallas kernels  14.9 us (14%)
  between operations  1.54 us (1%)
    all_to_all x1, blocking collectives, body(): lax.all_to_all(shares.reshape(C * blocks, -1, HD), ('c', 'head'), 0, 0, t...  17.8 us
    all_to_all x1, blocking collectives, body(): queries = lax.all_to_all(part, CHIPS, 0, 0, tiled=True)  17.3 us
    all_to_all x1, waiting for transfers between devices, body(): from_chips = lax.all_to_all(to_chips, CHIPS, 0, 0, tiled=True)  9.6 us
    pallas_call x2, Pallas kernels, encode(): pl.pallas_call(encode_kernel, out_shape=jax.ShapeDtypeStruct(query.shape,...  9.07 us
    all_to_all x1, starting transfers between devices, body(): from_chips = lax.all_to_all(to_chips, CHIPS, 0, 0, tiled=True)  8.6 us
    ppermute x1, waiting for transfers between devices, with_anchor(): return pack_anchor(key, lax.ppermute(value, 'c', [(0, 1)]), packed)  7.9 us
    all_to_all x1, starting transfers between devices, body(): gathered = lax.all_to_all(merge(met), CHIPS, 0, 0, tiled=True)  6.47 us
    all_to_all x1, waiting for transfers between devices, body(): gathered = lax.all_to_all(merge(met), CHIPS, 0, 0, tiled=True)  5.69 us
  transfers between devices with their start and end apart: 5, of which 4 were waited for; matrix products, arithmetic and copies ran while one was open for 0% of the time, Pallas kernels for 8%

profile of v5, /device:TPU:1, one launch (start us, length us, event | category | flops | bytes accessed | tf_op | source)
XLA Modules:
  0.0 108.8 jit_solution(17513335569212165332)
XLA Ops:
  1.3 10.1 %conditional.1 = (bf16[8,4,48,128]{3,2,1,0:T(8,128)(2,1)}) conditional(s32[]{:T(128)} %clamp.3, () %tuple.29, bf16[256,1024]{1,0:T(8,128)(2,1)} %param.18, bf16[256,1024]{1,0:T(8,128)(2,1)} %param.18, (bf16[512,128]{1,0:T(8,128)(2,1)}, bf16[512,128]{1,0:T(8,128)(2,1)}) %tuple.30, (bf16[512,128]{1,0:T(8,128)(2,1)}, ...), branch_computations={%region_0.1_spmd, %region_1.2_spmd, %region_2.3_spmd, %region_3.4_... | conditional | bytes 3145844 | solution.py:450
  1.4 0.0 copy-start.5
  1.4 1.4 %collective-permute-start.2 = (bf16[512,128]{1,0:T(8,128)(2,1)}, bf16[512,128]{1,0:T(8,128)(2,1)S(1)}, u32[]{:S(2)}, u32[]{:S(2)}) collective-permute-start(bf16[512,128]{1,0:T(8,128)(2,1)} %get-tuple-element.22), channel_id=1, source_target_pairs={{0,8},{1,9},{2,10},{3,11},{4,12},{5,13},{6,14},{7,15},{16,24},{17,... | collective-permute-start | bytes 393224 | tf_op jit(solution)/shard_map/cond/branch_3_fun/ppermute | solution.py:433
  2.8 7.9 %collective-permute-done.2.value = bf16[512,128]{1,0:T(8,128)(2,1)S(1)} collective-permute-done((bf16[512,128]{1,0:T(8,128)(2,1)}, bf16[512,128]{1,0:T(8,128)(2,1)S(1)}, u32[]{:S(2)}, u32[]{:S(2)}) %collective-permute-start.2) | collective-permute-done | bytes 131104 | tf_op jit(solution)/shard_map/cond/branch_3_fun/ppermute | solution.py:433
  10.7 0.0 copy-done.5
  10.7 0.7 pack_anchor.3
  11.4 0.0 copy-start
  11.4 0.0 copy-start.8
  11.4 8.6 %all-to-all-start = ((bf16[32,48,128]{2,1,0:T(8,128)(2,1)}), bf16[32,48,128]{2,1,0:T(8,128)(2,1)S(1)}, u32[]{:S(2)}, u32[]{:S(2)}) async-start(bf16[32,48,128]{2,1,0:T(8,128)(2,1)} %bitcast.1), calls=%async_computation | async-start | bytes 786432 | tf_op jit(solution)/shard_map/all_to_all | solution.py:452
  20.0 0.0 copy-done
  20.1 0.0 copy-start.1
  20.1 0.0 copy-start.2
  20.1 0.0 copy-start.4
  20.1 2.1 %collective-permute-start.7 = (bf16[512,128]{1,0:T(8,128)(2,1)S(1)}, bf16[512,128]{1,0:T(8,128)(2,1)S(1)}, u32[]{:S(2)}, u32[]{:S(2)}) collective-permute-start(bf16[512,128]{1,0:T(8,128)(2,1)S(1)} %constant_dynamic-slice_fusion), channel_id=1, source_target_pairs={{0,8},{8,0},{1,9},{9,1},{2,10},{10,2},{3,11},{11,3},{4,12},{12,4},... | collective-permute-start | bytes 393224 | tf_op jit(solution)/shard_map/ppermute | solution.py:455
  22.2 0.0 copy-done.8
  22.2 0.0 copy-done.1
  22.2 0.0 copy-done.2
  22.2 0.0 copy-done.4
  22.2 2.5 %all-gather = bf16[3072,128]{1,0:T(8,128)(2,1)S(1)} all-gather(bf16[1536,128]{1,0:T(8,128)(2,1)S(1)} %join.1), channel_id=2, replica_groups=mesh['z'=8,'x'=4,'c'=2,'head'=8] {'c'}, dimensions={0}, use_global_device_ids=true | all-gather | bytes 1179648 | tf_op jit(solution)/shard_map/all_gather | solution.py:453
  24.7 0.0 copy-start.9
  24.7 0.7 copy-done.9
  25.4 0.1 dynamic_slice.7
  25.5 0.1 pad_add_fusion.meta
  25.6 0.0 collective-permute-done.7.other
  25.6 9.6 %all-to-all-done.asked.anchor = bf16[32,48,128]{2,1,0:T(8,128)(2,1)S(1)} async-done(((bf16[32,48,128]{2,1,0:T(8,128)(2,1)}), bf16[32,48,128]{2,1,0:T(8,128)(2,1)S(1)}, u32[]{:S(2)}, u32[]{:S(2)}) %all-to-all-start) | async-done | bytes 393248 | tf_op jit(solution)/shard_map/all_to_all | solution.py:452
  35.2 0.1 spread.1
  35.3 17.3 %all_to_all.25 = bf16[32,48,128]{2,1,0:T(8,128)(2,1)S(1)} all-to-all(bf16[32,48,128]{2,1,0:T(8,128)(2,1)S(1)} %spread.1), channel_id=1, replica_groups=mesh['z'=8,'x'=4,'c'=2,'head'=8] {'z','x'}, dimensions={0} | all-to-all | bytes 786432 | tf_op jit(solution)/shard_map/all_to_all | solution.py:461
  52.5 3.1 %ask.1 = bf16[8,4,40,128]{3,2,1,0:T(8,128)(2,1)} custom-call(s32[5]{0:T(128)S(1)} %pad_add_fusion.meta, bf16[8,4,48,128]{3,2,1,0:T(8,128)(2,1)S(1)} %bitcast.17, bf16[2,1536,128]{2,1,0:T(8,128)(2,1)S(1)} %bitcast.16), custom_call_target="tpu_custom_call" | custom-call | flops 805306368 | bytes 1048576 | tf_op jit(solution)/shard_map/ask/pallas_call | solution.py:284
  55.6 0.0 copy-start.3
  55.6 5.5 %all-to-all-start.2 = ((bf16[32,40,128]{2,1,0:T(8,128)(2,1)}), bf16[32,40,128]{2,1,0:T(8,128)(2,1)S(1)}, u32[]{:S(2)}, u32[]{:S(2)}) async-start(bf16[32,40,128]{2,1,0:T(8,128)(2,1)} %bitcast.6), calls=%async_computation.2 | async-start | bytes 655360 | tf_op jit(solution)/shard_map/all_to_all | solution.py:464
  61.2 3.4 %all_gather.11.anchor = bf16[1024,128]{1,0:T(8,128)(2,1)S(1)} all-gather(bf16[512,128]{1,0:T(8,128)(2,1)S(1)} %bitcast.19), channel_id=1, replica_groups=mesh['z'=8,'x'=4,'c'=2,'head'=8] {'c'}, dimensions={0}, use_global_device_ids=true | all-gather | bytes 393216 | tf_op jit(solution)/shard_map/all_gather | solution.py:465
  64.6 0.0 copy-done.3
  64.6 4.5 %encode.2.rest_0_ = bf16[512,1024]{1,0:T(8,128)(2,1)} custom-call(s32[5]{0:T(128)S(1)} %pad_add_fusion.meta, bf16[512,1024]{1,0:T(8,128)(2,1)S(1)} %copy-done.3, bf16[512,128]{1,0:T(8,128)(2,1)S(1)} %copy-done.4, bf16[512,128]{1,0:T(8,128)(2,1)S(1)} %copy-done.8, bf16[1024,128]{1,0:T(8,128)(2,1)S(1)} %all_gather.11.anchor), custom_call_target="tpu_custom_call" | custom-call | flops 1342177280 | bytes 1310720 | tf_op jit(solution)/shard_map/encode/pallas_call | solution.py:391
  69.1 3.2 %all-to-all-done.2.received = bf16[32,40,128]{2,1,0:T(8,128)(2,1)S(1)} async-done(((bf16[32,40,128]{2,1,0:T(8,128)(2,1)}), bf16[32,40,128]{2,1,0:T(8,128)(2,1)S(1)}, u32[]{:S(2)}, u32[]{:S(2)}) %all-to-all-start.2) | async-done | bytes 327712 | tf_op jit(solution)/shard_map/all_to_all | solution.py:464
  72.3 1.1 merge.1
  73.4 6.5 %all-to-all-start.3 = ((bf16[32,32,128]{2,1,0:T(8,128)(2,1)}), bf16[32,32,128]{2,1,0:T(8,128)(2,1)S(1)}, u32[]{:S(2)}, u32[]{:S(2)}) async-start(bf16[32,32,128]{2,1,0:T(8,128)(2,1)} %merge.1), calls=%async_computation.3 | async-start | bytes 524288 | tf_op jit(solution)/shard_map/all_to_all | solution.py:469
  79.9 4.5 %encode.3 = bf16[512,1024]{1,0:T(8,128)(2,1)} custom-call(s32[5]{0:T(128)S(1)} %pad_add_fusion.meta, bf16[512,1024]{1,0:T(8,128)(2,1)S(1)} %copy-done.3, bf16[512,128]{1,0:T(8,128)(2,1)S(1)} %copy-done.4, bf16[512,128]{1,0:T(8,128)(2,1)S(1)} %copy-done.8, bf16[1024,128]{1,0:T(8,128)(2,1)S(1)} %all_gather.11.anchor, ...), custom_call_target="tpu_custom_call", output_to_operand_aliasing={{}: (5, {})} | custom-call | flops 1342177280 | bytes 1310720 | tf_op jit(solution)/shard_map/encode/pallas_call | solution.py:391
  84.4 5.7 %all-to-all-done.3 = bf16[32,32,128]{2,1,0:T(8,128)(2,1)S(1)} async-done(((bf16[32,32,128]{2,1,0:T(8,128)(2,1)}), bf16[32,32,128]{2,1,0:T(8,128)(2,1)S(1)}, u32[]{:S(2)}, u32[]{:S(2)}) %all-to-all-start.3) | async-done | bytes 262176 | tf_op jit(solution)/shard_map/all_to_all | solution.py:469
  90.1 0.3 project.1
  90.4 17.8 %all_to_all.26.shares = bf16[16,32,128]{2,1,0:T(8,128)(2,1)S(1)} all-to-all(bf16[16,32,128]{2,1,0:T(8,128)(2,1)S(1)} %bitcast.18), channel_id=1, replica_groups=mesh['z'=8,'x'=4,'c'=2,'head'=8] {'c','head'}, dimensions={0} | all-to-all | bytes 262144 | tf_op jit(solution)/shard_map/all_to_all | solution.py:474
  108.2 0.6 total.1
  (4 shorter events, 0.1 us)
Async XLA Ops:
  1.4 9.4 %copy-start.5 = (bf16[512,128]{1,0:T(8,128)(2,1)S(1)}, bf16[512,128]{1,0:T(8,128)(2,1)}, u32[]{:S(2)}) copy-start(bf16[512,128]{1,0:T(8,128)(2,1)} %get-tuple-element.21.key) | copy-start | bytes 393220 | tf_op jit(solution)/shard_map/cond
  1.4 9.3 %collective-permute-start.2 = (bf16[512,128]{1,0:T(8,128)(2,1)}, bf16[512,128]{1,0:T(8,128)(2,1)S(1)}, u32[]{:S(2)}, u32[]{:S(2)}) collective-permute-start(bf16[512,128]{1,0:T(8,128)(2,1)} %get-tuple-element.22), channel_id=1, source_target_pairs={{0,8},{1,9},{2,10},{3,11},{4,12},{5,13},{6,14},{7,15},{16,24},{17,... | collective-permute-start | bytes 393224 | tf_op jit(solution)/shard_map/cond/branch_3_fun/ppermute | solution.py:433
  11.4 8.6 %copy-start = (bf16[1024,128]{1,0:T(8,128)(2,1)S(1)}, bf16[1024,128]{1,0:T(8,128)(2,1)}, u32[]{:S(2)}) copy-start(bf16[1024,128]{1,0:T(8,128)(2,1)} %weight.1) | copy-start | bytes 786436
  11.4 10.8 %copy-start.8 = (bf16[512,128]{1,0:T(8,128)(2,1)S(1)}, bf16[512,128]{1,0:T(8,128)(2,1)}, u32[]{:S(2)}) copy-start(bf16[512,128]{1,0:T(8,128)(2,1)} %value.3) | copy-start | bytes 393220
  11.4 23.8 %all-to-all-start = ((bf16[32,48,128]{2,1,0:T(8,128)(2,1)}), bf16[32,48,128]{2,1,0:T(8,128)(2,1)S(1)}, u32[]{:S(2)}, u32[]{:S(2)}) async-start(bf16[32,48,128]{2,1,0:T(8,128)(2,1)} %bitcast.1), calls=%async_computation | async-start | bytes 786432 | tf_op jit(solution)/shard_map/all_to_all | solution.py:452
  20.1 2.1 %copy-start.1 = (bf16[256,128]{1,0:T(8,128)(2,1)S(1)}, bf16[256,128]{1,0:T(8,128)(2,1)}, u32[]{:S(2)}) copy-start(bf16[256,128]{1,0:T(8,128)(2,1)} %refs_2_.1) | copy-start | bytes 196612
  20.1 2.1 %copy-start.2 = (bf16[256,128]{1,0:T(8,128)(2,1)S(1)}, bf16[256,128]{1,0:T(8,128)(2,1)}, u32[]{:S(2)}) copy-start(bf16[256,128]{1,0:T(8,128)(2,1)} %refs_3_.1) | copy-start | bytes 196612
  20.1 2.1 %copy-start.4 = (bf16[512,128]{1,0:T(8,128)(2,1)S(1)}, bf16[512,128]{1,0:T(8,128)(2,1)}, u32[]{:S(2)}) copy-start(bf16[512,128]{1,0:T(8,128)(2,1)} %key.3) | copy-start | bytes 393220
  20.1 5.5 %collective-permute-start.7 = (bf16[512,128]{1,0:T(8,128)(2,1)S(1)}, bf16[512,128]{1,0:T(8,128)(2,1)S(1)}, u32[]{:S(2)}, u32[]{:S(2)}) collective-permute-start(bf16[512,128]{1,0:T(8,128)(2,1)S(1)} %constant_dynamic-slice_fusion), channel_id=1, source_target_pairs={{0,8},{8,0},{1,9},{9,1},{2,10},{10,2},{3,11},{11,3},{4,12},{12,4},... | collective-permute-start | bytes 393224 | tf_op jit(solution)/shard_map/ppermute | solution.py:455
  24.7 0.7 copy-start.9
  55.6 9.0 %copy-start.3 = (bf16[512,1024]{1,0:T(8,128)(2,1)S(1)}, bf16[512,1024]{1,0:T(8,128)(2,1)}, u32[]{:S(2)}) copy-start(bf16[512,1024]{1,0:T(8,128)(2,1)} %query.5) | copy-start | bytes 3145732
  55.6 16.7 %all-to-all-start.2 = ((bf16[32,40,128]{2,1,0:T(8,128)(2,1)}), bf16[32,40,128]{2,1,0:T(8,128)(2,1)S(1)}, u32[]{:S(2)}, u32[]{:S(2)}) async-start(bf16[32,40,128]{2,1,0:T(8,128)(2,1)} %bitcast.6), calls=%async_computation.2 | async-start | bytes 655360 | tf_op jit(solution)/shard_map/all_to_all | solution.py:464
  73.4 16.7 %all-to-all-start.3 = ((bf16[32,32,128]{2,1,0:T(8,128)(2,1)}), bf16[32,32,128]{2,1,0:T(8,128)(2,1)S(1)}, u32[]{:S(2)}, u32[]{:S(2)}) async-start(bf16[32,32,128]{2,1,0:T(8,128)(2,1)} %merge.1), calls=%async_computation.3 | async-start | bytes 524288 | tf_op jit(solution)/shard_map/all_to_all | solution.py:469
